TPU v7x, 32 devices: a whole 2x2x4 slice. The times are simulated.
32 devices in a mesh: vid: 16 (over z, y, core), aud: 2 (over x).
Axes of the slice: x: 2, y: 2, z: 4, core: 2. Of those that a mesh axis runs over, the one named last changes fastest.
Arguments:
- q_video: bfloat16 [4096, 1536], P('vid', 'aud'), may hold values from -240 to 240
- video_key_rows: bfloat16 [4096, 1536], P('vid', 'aud'), may hold values from -6 to 6
- video_value_rows: bfloat16 [4096, 1536], P('vid', 'aud'), may hold values from -6 to 6
- g_video: bfloat16 [4096, 1536], P('vid', 'aud'), may hold values from -6 to 6
- q_audio: bfloat16 [1024, 1536], P(('vid', 'aud')), may hold values from -240 to 240
- k_audio: bfloat16 [1024, 1536], P(('vid', 'aud')), may hold values from -6 to 6
- v_audio: bfloat16 [1024, 1536], P(('vid', 'aud')), may hold values from -6 to 6
- g_audio: bfloat16 [1024, 1536], P(('vid', 'aud')), may hold values from -6 to 6
- window: int32 [64, 2], replicated, may hold values from 0 to 15, as said below
- audio_len: int32 [16], replicated, may hold values from 1 to 64
Outputs:
- out_video: bfloat16 [4096, 1536], P('vid', 'aud')
- out_audio: bfloat16 [1024, 1536], P(('vid', 'aud'))
- dq_video: bfloat16 [4096, 1536], P('vid', 'aud')
- dk_video: bfloat16 [4096, 1536], P('vid', 'aud')
- dv_video: bfloat16 [4096, 1536], P('vid', 'aud')
- dq_audio: bfloat16 [1024, 1536], P(('vid', 'aud'))
- dk_audio: bfloat16 [1024, 1536], P(('vid', 'aud'))
- dv_audio: bfloat16 [1024, 1536], P(('vid', 'aud'))
Inputs may be any that keep to these rules, and one draw needn't show every extreme that they name: window[i] = (start, count) with 1 <= count <= 3 (3 is reached in every draw), start <= i // 4 < start + count, and start + count <= 16.
All inputs are finite; a program needn't handle non-finite values.
Results may differ from a plain program's by a relative error of at most 0.0095.
Values may be sent and summed in bfloat16 or wider, within the bound.
A program may use at most 64 MiB of HBM per device.

v0:
```python
import jax
import jax.numpy as jnp
from jax import lax
from jax.sharding import PartitionSpec as P

HD = 64
BLK = 64
WMAX = 3


NEG_FILL = -1e30


def from_behind(value, axis, steps):
    count = lax.axis_size(axis)
    leading, last = (max(0, -steps), min(count, count - steps))
    return lax.ppermute(value, axis, [(source, source + steps) for source in range(leading, last)])


def split_heads(matrix):
    return matrix.reshape(matrix.shape[0], matrix.shape[1] // HD, HD)


def join_heads(tensor):
    return tensor.reshape(tensor.shape[0], -1)


def masked_scores(queries, key_rows, allowed):
    scores = jnp.einsum(
        "rhd,khd->hrk",
        split_heads(queries),
        split_heads(key_rows),
        preferred_element_type=jnp.float32,
    )
    return jnp.where(allowed[None], scores * HD ** (-0.5), NEG_FILL)


def head_delta(cotangent, out_rows):
    return jnp.sum(
        split_heads(cotangent).astype(jnp.float32) * split_heads(out_rows).astype(jnp.float32),
        axis=2,
    )


def gradient_terms(queries, key_rows, value_rows, cotangent, attention_probs, weights_b, deltas):
    scale = HD ** (-0.5)
    g_heads = split_heads(cotangent)
    grad_p = jnp.einsum(
        "rhd,khd->hrk", g_heads, split_heads(value_rows), preferred_element_type=jnp.float32
    )
    grad_s = (attention_probs * (grad_p - deltas.T[:, :, None])).astype(jnp.bfloat16)
    grad_q = (
        jnp.einsum(
            "hrk,khd->rhd", grad_s, split_heads(key_rows), preferred_element_type=jnp.float32
        )
        * scale
    )
    grad_k = (
        jnp.einsum("hrk,rhd->khd", grad_s, split_heads(queries), preferred_element_type=jnp.float32)
        * scale
    )
    grad_v = jnp.einsum("hrk,rhd->khd", weights_b, g_heads, preferred_element_type=jnp.float32)
    return (join_heads(grad_q), join_heads(grad_k), join_heads(grad_v))


def full_attention(queries, key_rows, value_rows, cotangent, allowed, query_valid):
    scores = masked_scores(queries, key_rows, allowed)
    row_max = jnp.max(scores, axis=2, keepdims=True)
    row_sum = jnp.sum(
        jnp.where(allowed[None], jnp.exp(scores - row_max), 0.0), axis=2, keepdims=True
    )
    attention_probs = jnp.where(allowed[None], jnp.exp(scores - (row_max + jnp.log(row_sum))), 0.0)
    weights_b = attention_probs.astype(jnp.bfloat16)
    mixed = jnp.einsum(
        "hrk,khd->rhd", weights_b, split_heads(value_rows), preferred_element_type=jnp.float32
    )
    out_rows = join_heads(mixed * query_valid[:, None, None]).astype(jnp.bfloat16)
    deltas = head_delta(cotangent, out_rows)
    grad_q, grad_k, grad_v = gradient_terms(
        queries, key_rows, value_rows, cotangent, attention_probs, weights_b, deltas
    )
    return (out_rows, grad_q, grad_k, grad_v)


def body(
    q_video,
    video_key_rows,
    video_value_rows,
    g_video,
    q_audio,
    k_audio,
    v_audio,
    g_audio,
    window,
    audio_len,
):
    q_aud, k_aud, v_aud, g_aud = (
        lax.all_to_all(q_audio, "aud", split_axis=1, concat_axis=0, tiled=True),
        lax.all_to_all(k_audio, "aud", split_axis=1, concat_axis=0, tiled=True),
        lax.all_to_all(v_audio, "aud", split_axis=1, concat_axis=0, tiled=True),
        lax.all_to_all(g_audio, "aud", split_axis=1, concat_axis=0, tiled=True),
    )
    video_rows = q_video.shape[0]
    audio_rows = q_aud.shape[0]
    video_blocks = video_rows // BLK
    audio_blocks = audio_rows // BLK
    reach_dev = (WMAX - 2 + audio_blocks) // audio_blocks
    near_count = 2 * reach_dev + 1
    offsets = [
        window_shift for window_shift in range(-reach_dev, reach_dev + 1) if window_shift != 0
    ]
    devices = lax.axis_size("vid")
    device = lax.axis_index("vid")
    audio_total = audio_len.shape[0]

    def nearby_row_span(pieces, axis):
        return jnp.concatenate(
            [pieces[window_shift] for window_shift in range(-reach_dev, reach_dev + 1)], axis=axis
        )

    def rows_of(tensor, window_shift, size, axis):
        return lax.slice_in_dim(
            tensor,
            (window_shift + reach_dev) * size,
            (window_shift + reach_dev + 1) * size,
            axis=axis,
        )

    own_lens = lax.dynamic_slice_in_dim(audio_len, device * audio_blocks, audio_blocks, 0)
    audio_valid = (jnp.arange(audio_rows) % BLK < jnp.repeat(own_lens, BLK)).astype(jnp.float32)
    g_masked = g_aud * audio_valid[:, None].astype(jnp.bfloat16)
    own_window = lax.dynamic_slice_in_dim(window, device * video_blocks, video_blocks, 0)
    near_ablk = (device - reach_dev) * audio_blocks + jnp.arange(near_count * audio_blocks)
    block_ok = (near_ablk[None] >= own_window[:, 0:1]) & (
        near_ablk[None] < own_window[:, 0:1] + own_window[:, 1:2]
    )
    window_tok = jnp.repeat(jnp.repeat(block_ok, BLK, 0), BLK, 1)
    near_lens = jnp.sum(
        jnp.where(near_ablk[:, None] == jnp.arange(audio_total)[None], audio_len[None], 0), axis=1
    )
    key_ok = jnp.arange(near_count * audio_rows) % BLK < jnp.repeat(near_lens, BLK)
    allowed_va = window_tok & key_ok[None]
    video_ones = jnp.ones((video_rows,), jnp.float32)
    pieces = {0: (k_aud, v_aud, q_aud, g_masked)}
    for window_shift in offsets:
        pieces[window_shift] = from_behind((k_aud, v_aud, q_aud, g_masked), "vid", -window_shift)
    gathered = [
        nearby_row_span({window_shift: pieces[window_shift][member] for window_shift in pieces}, 0)
        for member in range(4)
    ]
    out_video, dq_video, dk_near, dv_near = full_attention(
        q_video, gathered[0], gathered[1], g_video, allowed_va, video_ones
    )
    allowed_kv = window_tok.T
    scores = masked_scores(gathered[2], video_key_rows, allowed_kv)
    part_max = jnp.max(scores, axis=2)
    part_sum = jnp.sum(
        jnp.where(allowed_kv[None], jnp.exp(scores - part_max[:, :, None]), 0.0), axis=2
    )
    own_max = rows_of(part_max, 0, audio_rows, 1)
    own_sum = rows_of(part_sum, 0, audio_rows, 1)
    for window_shift in offsets:
        max_in, sum_in = from_behind(
            (
                rows_of(part_max, window_shift, audio_rows, 1),
                rows_of(part_sum, window_shift, audio_rows, 1),
            ),
            "vid",
            window_shift,
        )
        source = device - window_shift
        present = (source >= 0) & (source < devices)
        max_in = jnp.where(present, max_in, NEG_FILL)
        sum_in = jnp.where(present, sum_in, 0.0)
        merged = jnp.maximum(own_max, max_in)
        own_sum = own_sum * jnp.exp(own_max - merged) + sum_in * jnp.exp(max_in - merged)
        own_max = merged
    own_lse = own_max + jnp.log(own_sum)
    lse_pieces = {0: own_lse}
    for window_shift in offsets:
        lse_pieces[window_shift] = from_behind(own_lse, "vid", -window_shift)
    near_lse = nearby_row_span(lse_pieces, 1)
    attention_probs = jnp.where(allowed_kv[None], jnp.exp(scores - near_lse[:, :, None]), 0.0)
    weights_b = attention_probs.astype(jnp.bfloat16)
    partial_value = join_heads(
        jnp.einsum(
            "hrk,khd->rhd",
            weights_b,
            split_heads(video_value_rows),
            preferred_element_type=jnp.float32,
        )
    )
    summed = rows_of(partial_value, 0, audio_rows, 0)
    for window_shift in offsets:
        summed = summed + from_behind(
            rows_of(partial_value, window_shift, audio_rows, 0), "vid", window_shift
        )
    out_aud = (summed * audio_valid[:, None]).astype(jnp.bfloat16)
    own_delta = head_delta(g_masked, out_aud)
    delta_pieces = {0: own_delta}
    for window_shift in offsets:
        delta_pieces[window_shift] = from_behind(own_delta, "vid", -window_shift)
    near_delta = nearby_row_span(delta_pieces, 0)
    dq_near, dk_video, dv_video = gradient_terms(
        gathered[2],
        video_key_rows,
        video_value_rows,
        gathered[3],
        attention_probs,
        weights_b,
        near_delta,
    )
    dk_aud = rows_of(dk_near, 0, audio_rows, 0)
    dv_aud = rows_of(dv_near, 0, audio_rows, 0)
    dq_aud = rows_of(dq_near, 0, audio_rows, 0)
    for window_shift in offsets:
        dk_in, dv_in, dq_in = from_behind(
            (
                rows_of(dk_near, window_shift, audio_rows, 0),
                rows_of(dv_near, window_shift, audio_rows, 0),
                rows_of(dq_near, window_shift, audio_rows, 0),
            ),
            "vid",
            window_shift,
        )
        dk_aud = dk_aud + dk_in
        dv_aud = dv_aud + dv_in
        dq_aud = dq_aud + dq_in
    results = (
        lax.all_to_all(out_aud, "aud", split_axis=0, concat_axis=1, tiled=True),
        lax.all_to_all(dq_aud.astype(jnp.bfloat16), "aud", split_axis=0, concat_axis=1, tiled=True),
        lax.all_to_all(dk_aud.astype(jnp.bfloat16), "aud", split_axis=0, concat_axis=1, tiled=True),
        lax.all_to_all(dv_aud.astype(jnp.bfloat16), "aud", split_axis=0, concat_axis=1, tiled=True),
    )
    return (
        out_video,
        results[0],
        dq_video.astype(jnp.bfloat16),
        dk_video.astype(jnp.bfloat16),
        dv_video.astype(jnp.bfloat16),
        results[1],
        results[2],
        results[3],
    )


def solution(mesh):
    in_specs = (
        P("vid", "aud"),
        P("vid", "aud"),
        P("vid", "aud"),
        P("vid", "aud"),
        P(("vid", "aud"), None),
        P(("vid", "aud"), None),
        P(("vid", "aud"), None),
        P(("vid", "aud"), None),
        P(),
        P(),
    )
    out_specs = (
        P("vid", "aud"),
        P(("vid", "aud"), None),
        P("vid", "aud"),
        P("vid", "aud"),
        P("vid", "aud"),
        P(("vid", "aud"), None),
        P(("vid", "aud"), None),
        P(("vid", "aud"), None),
    )
    return jax.shard_map(body, mesh=mesh, in_specs=in_specs, out_specs=out_specs, check_vma=False)
```

profile of v0, /device:TPU:12, one launch (start us, length us, event | category | flops | bytes accessed | tf_op | source)
XLA Modules:
  0.0 284.5 jit_solution(13612878907126887607)
XLA Ops:
  2.2 3.3 %all-to-all-start.1 = ((bf16[32,2,768]{2,0,1:T(8,128)(2,1)}), bf16[32,2,768]{2,0,1:T(8,128)(2,1)S(1)}, u32[]{:S(2)}, u32[]{:S(2)}) async-start(bf16[32,2,768]{2,0,1:T(8,128)(2,1)} %bitcast.152), calls=%async_computation.1 | async-start | bytes 196608 | tf_op jit(solution)/shard_map/all_to_all | solution.py:99
  9.9 3.3 %all-to-all-start = ((bf16[32,2,768]{2,0,1:T(8,128)(2,1)}), bf16[32,2,768]{2,0,1:T(8,128)(2,1)S(1)}, u32[]{:S(2)}, u32[]{:S(2)}) async-start(bf16[32,2,768]{2,0,1:T(8,128)(2,1)} %bitcast.153), calls=%async_computation | async-start | bytes 196608 | tf_op jit(solution)/shard_map/all_to_all | solution.py:100
  17.5 3.3 %all-to-all-start.4 = ((bf16[32,2,768]{2,0,1:T(8,128)(2,1)}), bf16[32,2,768]{2,0,1:T(8,128)(2,1)S(1)}, u32[]{:S(2)}, u32[]{:S(2)}) async-start(bf16[32,2,768]{2,0,1:T(8,128)(2,1)} %bitcast.150), calls=%async_computation.4 | async-start | bytes 196608 | tf_op jit(solution)/shard_map/all_to_all | solution.py:101
  28.4 2.4 collective-permute-start.7
  32.7 2.4 collective-permute-start.5
  35.1 4.3 %collective-permute-start.4 = (bf16[64,768]{1,0:T(8,128)(2,1)S(1)}, bf16[64,768]{1,0:T(8,128)(2,1)S(1)}, u32[]{:S(2)}, u32[]{:S(2)}) collective-permute-start(bf16[64,768]{1,0:T(8,128)(2,1)S(1)} %bitcast.213), channel_id=1, source_target_pairs={{0,4},{2,6},{4,8},{6,10},{8,12},{10,14},{12,16},{14,18},{16,20},{1... | collective-permute-start | bytes 294920 | tf_op jit(solution)/shard_map/ppermute | solution.py:17
  41.4 4.0 %all-to-all-start.2 = ((bf16[32,2,768]{2,0,1:T(8,128)(2,1)}), bf16[32,2,768]{2,0,1:T(8,128)(2,1)}, u32[]{:S(2)}, u32[]{:S(2)}) async-start(bf16[32,2,768]{2,0,1:T(8,128)(2,1)} %bitcast.151), calls=%async_computation.2 | async-start | bytes 196608 | tf_op jit(solution)/shard_map/all_to_all | solution.py:98
  47.8 2.2 all-to-all-done.2
  53.5 2.4 collective-permute-start.1
  56.1 4.6 %collective-permute-start = (bf16[64,768]{1,0:T(8,128)(2,1)S(1)}, bf16[64,768]{1,0:T(8,128)(2,1)S(1)}, u32[]{:S(2)}, u32[]{:S(2)}) collective-permute-start(bf16[64,768]{1,0:T(8,128)(2,1)S(1)} %bitcast.219), channel_id=1, source_target_pairs={{0,4},{2,6},{4,8},{6,10},{8,12},{10,14},{12,16},{14,18},{16,20},{1... | collective-permute-start | bytes 294920 | tf_op jit(solution)/shard_map/ppermute | solution.py:17
  65.2 2.2 convolution_bitcast_fusion
  67.3 2.9 %collective-permute-start.10 = (bf16[64,768]{1,0:T(8,128)(2,1)}, bf16[64,768]{1,0:T(8,128)(2,1)}, u32[]{:S(2)}, u32[]{:S(2)}) collective-permute-start(bf16[64,768]{1,0:T(8,128)(2,1)} %bitcast.23), channel_id=1, source_target_pairs={{2,0},{4,2},{6,4},{8,6},{10,8},{12,10},{14,12},{16,14},{18,16},{20... | collective-permute-start | bytes 294920 | tf_op jit(solution)/shard_map/ppermute | solution.py:17
  73.5 4.4 %collective-permute-start.8 = (bf16[64,768]{1,0:T(8,128)(2,1)}, bf16[64,768]{1,0:T(8,128)(2,1)}, u32[]{:S(2)}, u32[]{:S(2)}) collective-permute-start(bf16[64,768]{1,0:T(8,128)(2,1)} %bitcast.23), channel_id=1, source_target_pairs={{0,4},{2,6},{4,8},{6,10},{8,12},{10,14},{12,16},{14,18},{16,20},{1... | collective-permute-start | bytes 294920 | tf_op jit(solution)/shard_map/ppermute | solution.py:17
  81.6 4.2 %multiply_reduce_fusion = (f32[256,12]{0,1:T(8,128)S(1)}, bf16[12,64,256]{2,1,0:T(8,128)(2,1)}) fusion(bf16[256,12,64]{0,2,1:T(8,128)(2,1)} %bitcast.203, bf16[320,12,64]{0,2,1:T(8,128)(2,1)S(1)} %concatenate.56, f32[12,320,256]{2,1,0:T(8,128)} %copy-done.2, f32[12,256]{1,0:T(8,128)S(1)} %log_add_fusion, pred[256,320]{0,1:T(8,128)(4,1)S(1)} %bitcast_and_fusion), kind=kOutput, calls=%fused_computation.25 | convolution fusion | flops 131724288 | bytes 5316608 | tf_op jit(solution)/shard_map/hrk,khd->rhd/dot_general | solution.py:74
  89.8 3.4 %collective-permute-start.30 = (bf16[64,768]{1,0:T(8,128)(2,1)}, bf16[64,768]{1,0:T(8,128)(2,1)}, u32[]{:S(2)}, u32[]{:S(2)}) collective-permute-start(bf16[64,768]{1,0:T(8,128)(2,1)} %bitcast_multiply_fusion.1), channel_id=1, source_target_pairs={{2,0},{4,2},{6,4},{8,6},{10,8},{12,10},{14,12},{16,14},{18,16},{20... | collective-permute-start | bytes 294920 | tf_op jit(solution)/shard_map/ppermute | solution.py:17
  97.3 4.6 %collective-permute-start.28 = (bf16[64,768]{1,0:T(8,128)(2,1)}, bf16[64,768]{1,0:T(8,128)(2,1)}, u32[]{:S(2)}, u32[]{:S(2)}) collective-permute-start(bf16[64,768]{1,0:T(8,128)(2,1)} %bitcast_multiply_fusion.1), channel_id=1, source_target_pairs={{0,4},{2,6},{4,8},{6,10},{8,12},{10,14},{12,16},{14,18},{16,20},{1... | collective-permute-start | bytes 294920 | tf_op jit(solution)/shard_map/ppermute | solution.py:17
  111.9 4.8 %collective-permute-start.19 = (f32[12,64]{1,0:T(8,128)S(1)}, f32[12,64]{1,0:T(8,128)S(1)}, u32[]{:S(2)}, u32[]{:S(2)}) collective-permute-start(f32[12,64]{1,0:T(8,128)S(1)} %get-tuple-element.81), channel_id=1, source_target_pairs={{0,4},{2,6},{4,8},{6,10},{8,12},{10,14},{12,16},{14,18},{16,20},{1... | collective-permute-start | bytes 9224 | tf_op jit(solution)/shard_map/ppermute | solution.py:17
  123.3 3.6 %collective-permute-start.17 = (f32[12,64]{1,0:T(8,128)}, f32[12,64]{1,0:T(8,128)S(1)}, u32[]{:S(2)}, u32[]{:S(2)}) collective-permute-start(f32[12,64]{1,0:T(8,128)} %get-tuple-element.83), channel_id=1, source_target_pairs={{2,0},{4,2},{6,4},{8,6},{10,8},{12,10},{14,12},{16,14},{18,16},{20... | collective-permute-start | bytes 9224 | tf_op jit(solution)/shard_map/ppermute | solution.py:17
  128.4 2.4 collective-permute-start.12
  130.9 4.3 %collective-permute-start.15 = (f32[12,64]{1,0:T(8,128)}, f32[12,64]{1,0:T(8,128)S(1)}, u32[]{:S(2)}, u32[]{:S(2)}) collective-permute-start(f32[12,64]{1,0:T(8,128)} %get-tuple-element.77), channel_id=1, source_target_pairs={{0,4},{2,6},{4,8},{6,10},{8,12},{10,14},{12,16},{14,18},{16,20},{1... | collective-permute-start | bytes 9224 | tf_op jit(solution)/shard_map/ppermute | solution.py:17
  137.2 3.6 %collective-permute-start.13 = (f32[12,64]{1,0:T(8,128)S(1)}, f32[12,64]{1,0:T(8,128)S(1)}, u32[]{:S(2)}, u32[]{:S(2)}) collective-permute-start(f32[12,64]{1,0:T(8,128)S(1)} %get-tuple-element.79), channel_id=1, source_target_pairs={{2,0},{4,2},{6,4},{8,6},{10,8},{12,10},{14,12},{16,14},{18,16},{20... | collective-permute-start | bytes 9224 | tf_op jit(solution)/shard_map/ppermute | solution.py:17
  156.5 2.8 collective-permute-start.23
  159.3 3.4 %collective-permute-start.22 = (f32[12,64]{1,0:T(8,128)S(1)}, f32[12,64]{1,0:T(8,128)S(1)}, u32[]{:S(2)}, u32[]{:S(2)}) collective-permute-start(f32[12,64]{1,0:T(8,128)S(1)} %fusion.17), channel_id=1, source_target_pairs={{2,0},{4,2},{6,4},{8,6},{10,8},{12,10},{14,12},{16,14},{18,16},{20... | collective-permute-start | bytes 9224 | tf_op jit(solution)/shard_map/ppermute | solution.py:17
  164.6 2.9 %collective-permute-start.20 = (f32[12,64]{1,0:T(8,128)S(1)}, f32[12,64]{1,0:T(8,128)S(1)}, u32[]{:S(2)}, u32[]{:S(2)}) collective-permute-start(f32[12,64]{1,0:T(8,128)S(1)} %fusion.17), channel_id=1, source_target_pairs={{0,4},{2,6},{4,8},{6,10},{8,12},{10,14},{12,16},{14,18},{16,20},{1... | collective-permute-start | bytes 9224 | tf_op jit(solution)/shard_map/ppermute | solution.py:17
  174.2 3.1 %collective-permute-start.42 = (f32[64,768]{1,0:T(8,128)}, f32[64,768]{1,0:T(8,128)}, u32[]{:S(2)}, u32[]{:S(2)}) collective-permute-start(f32[64,768]{1,0:T(8,128)} %copy.291), channel_id=1, source_target_pairs={{0,2},{2,4},{4,6},{6,8},{8,10},{10,12},{12,14},{14,16},{16,18},{18... | collective-permute-start | bytes 589832 | tf_op jit(solution)/shard_map/ppermute | solution.py:17
  177.3 3.2 %collective-permute-start.43 = (f32[64,768]{1,0:T(8,128)}, f32[64,768]{1,0:T(8,128)}, u32[]{:S(2)}, u32[]{:S(2)}) collective-permute-start(f32[64,768]{1,0:T(8,128)} %copy.292), channel_id=1, source_target_pairs={{0,4},{2,6},{4,8},{6,10},{8,12},{10,14},{12,16},{14,18},{16,20},{1... | collective-permute-start | bytes 589832 | tf_op jit(solution)/shard_map/ppermute | solution.py:17
  180.6 2.6 collective-permute-start.40
  183.8 2.8 collective-permute-start.45
  187.4 3.2 %convolution_bitcast_fusion.1 = f32[320,12,64]{0,2,1:T(8,128)S(1)} fusion(bf16[256,12,64]{0,2,1:T(8,128)(2,1)} %bitcast.200, f32[12,320,256]{2,1,0:T(8,128)} %copy-done.1, f32[12,320]{1,0:T(8,128)S(1)} %concatenate.69, pred[320,256]{1,0:T(8,128)(4,1)S(1)} %bitcast.195), kind=kOutput, calls=%fused_computation.18 | convolution fusion | flops 130744320 | bytes 5405696 | tf_op jit(solution)/shard_map/hrk,khd->rhd/dot_general | solution.py:186
  192.5 2.5 collective-permute-start.25
  197.0 3.4 %collective-permute-start.27 = (f32[64,768]{1,0:T(8,128)S(1)}, f32[64,768]{1,0:T(8,128)S(1)}, u32[]{:S(2)}, u32[]{:S(2)}) collective-permute-start(f32[64,768]{1,0:T(8,128)S(1)} %copy.272), channel_id=1, source_target_pairs={{0,4},{2,6},{4,8},{6,10},{8,12},{10,14},{12,16},{14,18},{16,20},{1... | collective-permute-start | bytes 589832 | tf_op jit(solution)/shard_map/ppermute | solution.py:17
  200.4 2.5 collective-permute-start.24
  204.8 4.0 %all-to-all-start.6 = ((bf16[2,32,768]{2,1,0:T(8,128)(2,1)}), bf16[2,32,768]{2,1,0:T(8,128)(2,1)}, u32[]{:S(2)}, u32[]{:S(2)}) async-start(bf16[2,32,768]{2,1,0:T(8,128)(2,1)} %bitcast.67), calls=%async_computation.6 | async-start | bytes 196608 | tf_op jit(solution)/shard_map/all_to_all | solution.py:232
  208.8 2.9 %collective-permute-start.46 = (f32[64,768]{1,0:T(8,128)}, f32[64,768]{1,0:T(8,128)S(1)}, u32[]{:S(2)}, u32[]{:S(2)}) collective-permute-start(f32[64,768]{1,0:T(8,128)} %copy.297), channel_id=1, source_target_pairs={{0,2},{2,4},{4,6},{6,8},{8,10},{10,12},{12,14},{14,16},{16,18},{18... | collective-permute-start | bytes 589832 | tf_op jit(solution)/shard_map/ppermute | solution.py:17
  211.7 4.1 %collective-permute-start.47 = (f32[64,768]{1,0:T(8,128)}, f32[64,768]{1,0:T(8,128)S(1)}, u32[]{:S(2)}, u32[]{:S(2)}) collective-permute-start(f32[64,768]{1,0:T(8,128)} %copy.298), channel_id=1, source_target_pairs={{0,4},{2,6},{4,8},{6,10},{8,12},{10,14},{12,16},{14,18},{16,20},{1... | collective-permute-start | bytes 589832 | tf_op jit(solution)/shard_map/ppermute | solution.py:17
  219.9 4.3 %collective-permute-start.35 = (f32[64,12]{1,0:T(8,128)S(1)}, f32[64,12]{1,0:T(8,128)S(1)}, u32[]{:S(2)}, u32[]{:S(2)}) collective-permute-start(f32[64,12]{1,0:T(8,128)S(1)} %multiply_reduce_fusion.1), channel_id=1, source_target_pairs={{4,0},{6,2},{8,4},{10,6},{12,8},{14,10},{16,12},{18,14},{20,16},{2... | collective-permute-start | bytes 9224 | tf_op jit(solution)/shard_map/ppermute | solution.py:17
  224.2 2.8 collective-permute-start.34
  229.0 3.1 %collective-permute-start.32 = (f32[64,12]{1,0:T(8,128)S(1)}, f32[64,12]{1,0:T(8,128)S(1)}, u32[]{:S(2)}, u32[]{:S(2)}) collective-permute-start(f32[64,12]{1,0:T(8,128)S(1)} %multiply_reduce_fusion.1), channel_id=1, source_target_pairs={{0,4},{2,6},{4,8},{6,10},{8,12},{10,14},{12,16},{14,18},{16,20},{1... | collective-permute-start | bytes 9224 | tf_op jit(solution)/shard_map/ppermute | solution.py:17
  235.0 4.2 %multiply_convert_fusion = bf16[12,320,256]{2,1,0:T(8,128)(2,1)S(1)} fusion(f32[12,320,256]{2,1,0:T(8,128)} %copy-done.1, bf16[320,12,64]{0,2,1:T(8,128)(2,1)} %bitcast.198, bf16[256,12,64]{0,2,1:T(8,128)(2,1)} %bitcast.201, f32[12,320]{1,0:T(8,128)S(1)} %bitcast.228, f32[12,320]{1,0:T(8,128)S(1)} %concatenate.69, pred[320,256]{1,0:T(8,128)(4,1)S(1)} %bitcast.196), kind=kOutput, calls=%fused_computation.3 | convolution fusion | flops 132710400 | bytes 6895616 | tf_op jit(solution)/shard_map/rhd,khd->hrk/dot_general | solution.py:48
  247.3 3.4 %collective-permute-start.37 = (f32[64,768]{1,0:T(8,128)}, f32[64,768]{1,0:T(8,128)}, u32[]{:S(2)}, u32[]{:S(2)}) collective-permute-start(f32[64,768]{1,0:T(8,128)} %copy.284), channel_id=1, source_target_pairs={{2,0},{4,2},{6,4},{8,6},{10,8},{12,10},{14,12},{16,14},{18,16},{20... | collective-permute-start | bytes 589832 | tf_op jit(solution)/shard_map/ppermute | solution.py:17
  250.7 2.1 collective-permute-start.38
  252.8 3.1 %collective-permute-start.39 = (f32[64,768]{1,0:T(8,128)}, f32[64,768]{1,0:T(8,128)}, u32[]{:S(2)}, u32[]{:S(2)}) collective-permute-start(f32[64,768]{1,0:T(8,128)} %copy.286), channel_id=1, source_target_pairs={{0,4},{2,6},{4,8},{6,10},{8,12},{10,14},{12,16},{14,18},{16,20},{1... | collective-permute-start | bytes 589832 | tf_op jit(solution)/shard_map/ppermute | solution.py:17
  255.9 2.7 collective-permute-start.36
  258.7 4.0 %all-to-all-start.7 = ((bf16[2,32,768]{2,1,0:T(8,128)(2,1)}), bf16[2,32,768]{2,1,0:T(8,128)(2,1)}, u32[]{:S(2)}, u32[]{:S(2)}) async-start(bf16[2,32,768]{2,1,0:T(8,128)(2,1)} %bitcast.207), calls=%async_computation.7 | async-start | bytes 196608 | tf_op jit(solution)/shard_map/all_to_all | solution.py:233
  262.7 3.4 %convolution_convert_fusion = bf16[12,64,256]{2,1,0:T(8,128)(2,1)S(1)} fusion(bf16[320,12,64]{0,2,1:T(8,128)(2,1)} %bitcast.199, f32[12,320,256]{2,1,0:T(8,128)} %copy-done.1, f32[12,320]{1,0:T(8,128)S(1)} %concatenate.69, pred[320,256]{1,0:T(8,128)(4,1)S(1)} %bitcast.197), kind=kOutput, calls=%fused_computation.23 | convolution fusion | flops 130940928 | bytes 4914176 | tf_op jit(solution)/shard_map/hrk,rhd->khd/dot_general | solution.py:62
  267.5 3.3 %all-to-all-start.3 = ((bf16[2,32,768]{2,1,0:T(8,128)(2,1)}), bf16[2,32,768]{2,1,0:T(8,128)(2,1)S(1)}, u32[]{:S(2)}, u32[]{:S(2)}) async-start(bf16[2,32,768]{2,1,0:T(8,128)(2,1)} %bitcast.38), calls=%async_computation.3 | async-start | bytes 196608 | tf_op jit(solution)/shard_map/all_to_all | solution.py:230
  272.9 2.5 all-to-all-done.3
  275.3 3.3 %all-to-all-start.5 = ((bf16[2,32,768]{2,1,0:T(8,128)(2,1)}), bf16[2,32,768]{2,1,0:T(8,128)(2,1)S(1)}, u32[]{:S(2)}, u32[]{:S(2)}) async-start(bf16[2,32,768]{2,1,0:T(8,128)(2,1)} %bitcast.59), calls=%async_computation.5 | async-start | bytes 196608 | tf_op jit(solution)/shard_map/all_to_all | solution.py:231
  (201 shorter events, 124.2 us)
Async XLA Ops:
  17.5 23.9 %all-to-all-start.4 = ((bf16[32,2,768]{2,0,1:T(8,128)(2,1)}), bf16[32,2,768]{2,0,1:T(8,128)(2,1)S(1)}, u32[]{:S(2)}, u32[]{:S(2)}) async-start(bf16[32,2,768]{2,0,1:T(8,128)(2,1)} %bitcast.150), calls=%async_computation.4 | async-start | bytes 196608 | tf_op jit(solution)/shard_map/all_to_all | solution.py:101
  28.4 23.0 %collective-permute-start.7 = (bf16[64,768]{1,0:T(8,128)(2,1)S(1)}, bf16[64,768]{1,0:T(8,128)(2,1)S(1)}, u32[]{:S(2)}, u32[]{:S(2)}) collective-permute-start(bf16[64,768]{1,0:T(8,128)(2,1)S(1)} %bitcast.210), channel_id=1, source_target_pairs={{4,0},{6,2},{8,4},{10,6},{12,8},{14,10},{16,12},{18,14},{20,16},{2... | collective-permute-start | bytes 294920 | tf_op jit(solution)/shard_map/ppermute | solution.py:17
  30.8 22.7 %collective-permute-start.6 = (bf16[64,768]{1,0:T(8,128)(2,1)S(1)}, bf16[64,768]{1,0:T(8,128)(2,1)S(1)}, u32[]{:S(2)}, u32[]{:S(2)}) collective-permute-start(bf16[64,768]{1,0:T(8,128)(2,1)S(1)} %bitcast.211), channel_id=1, source_target_pairs={{2,0},{4,2},{6,4},{8,6},{10,8},{12,10},{14,12},{16,14},{18,16},{20... | collective-permute-start | bytes 294920 | tf_op jit(solution)/shard_map/ppermute | solution.py:17
  32.7 23.3 %collective-permute-start.5 = (bf16[64,768]{1,0:T(8,128)(2,1)S(1)}, bf16[64,768]{1,0:T(8,128)(2,1)S(1)}, u32[]{:S(2)}, u32[]{:S(2)}) collective-permute-start(bf16[64,768]{1,0:T(8,128)(2,1)S(1)} %bitcast.212), channel_id=1, source_target_pairs={{0,2},{2,4},{4,6},{6,8},{8,10},{10,12},{12,14},{14,16},{16,18},{18... | collective-permute-start | bytes 294920 | tf_op jit(solution)/shard_map/ppermute | solution.py:17
  35.1 25.7 %collective-permute-start.4 = (bf16[64,768]{1,0:T(8,128)(2,1)S(1)}, bf16[64,768]{1,0:T(8,128)(2,1)S(1)}, u32[]{:S(2)}, u32[]{:S(2)}) collective-permute-start(bf16[64,768]{1,0:T(8,128)(2,1)S(1)} %bitcast.213), channel_id=1, source_target_pairs={{0,4},{2,6},{4,8},{6,10},{8,12},{10,14},{12,16},{14,18},{16,20},{1... | collective-permute-start | bytes 294920 | tf_op jit(solution)/shard_map/ppermute | solution.py:17
  39.5 27.9 %collective-permute-start.3 = (bf16[64,768]{1,0:T(8,128)(2,1)S(1)}, bf16[64,768]{1,0:T(8,128)(2,1)S(1)}, u32[]{:S(2)}, u32[]{:S(2)}) collective-permute-start(bf16[64,768]{1,0:T(8,128)(2,1)S(1)} %bitcast.215), channel_id=1, source_target_pairs={{4,0},{6,2},{8,4},{10,6},{12,8},{14,10},{16,12},{18,14},{20,16},{2... | collective-permute-start | bytes 294920 | tf_op jit(solution)/shard_map/ppermute | solution.py:17
  51.4 19.0 %collective-permute-start.2 = (bf16[64,768]{1,0:T(8,128)(2,1)S(1)}, bf16[64,768]{1,0:T(8,128)(2,1)}, u32[]{:S(2)}, u32[]{:S(2)}) collective-permute-start(bf16[64,768]{1,0:T(8,128)(2,1)S(1)} %bitcast.217), channel_id=1, source_target_pairs={{2,0},{4,2},{6,4},{8,6},{10,8},{12,10},{14,12},{16,14},{18,16},{20... | collective-permute-start | bytes 294920 | tf_op jit(solution)/shard_map/ppermute | solution.py:17
  53.5 20.0 %collective-permute-start.1 = (bf16[64,768]{1,0:T(8,128)(2,1)S(1)}, bf16[64,768]{1,0:T(8,128)(2,1)}, u32[]{:S(2)}, u32[]{:S(2)}) collective-permute-start(bf16[64,768]{1,0:T(8,128)(2,1)S(1)} %bitcast.218), channel_id=1, source_target_pairs={{0,2},{2,4},{4,6},{6,8},{8,10},{10,12},{12,14},{14,16},{16,18},{18... | collective-permute-start | bytes 294920 | tf_op jit(solution)/shard_map/ppermute | solution.py:17
  56.1 22.9 %collective-permute-start = (bf16[64,768]{1,0:T(8,128)(2,1)S(1)}, bf16[64,768]{1,0:T(8,128)(2,1)S(1)}, u32[]{:S(2)}, u32[]{:S(2)}) collective-permute-start(bf16[64,768]{1,0:T(8,128)(2,1)S(1)} %bitcast.219), channel_id=1, source_target_pairs={{0,4},{2,6},{4,8},{6,10},{8,12},{10,14},{12,16},{14,18},{16,20},{1... | collective-permute-start | bytes 294920 | tf_op jit(solution)/shard_map/ppermute | solution.py:17
  60.8 29.0 %collective-permute-start.11 = (bf16[64,768]{1,0:T(8,128)(2,1)}, bf16[64,768]{1,0:T(8,128)(2,1)}, u32[]{:S(2)}, u32[]{:S(2)}) collective-permute-start(bf16[64,768]{1,0:T(8,128)(2,1)} %bitcast.23), channel_id=1, source_target_pairs={{4,0},{6,2},{8,4},{10,6},{12,8},{14,10},{16,12},{18,14},{20,16},{2... | collective-permute-start | bytes 294920 | tf_op jit(solution)/shard_map/ppermute | solution.py:17
  67.3 26.9 %collective-permute-start.10 = (bf16[64,768]{1,0:T(8,128)(2,1)}, bf16[64,768]{1,0:T(8,128)(2,1)}, u32[]{:S(2)}, u32[]{:S(2)}) collective-permute-start(bf16[64,768]{1,0:T(8,128)(2,1)} %bitcast.23), channel_id=1, source_target_pairs={{2,0},{4,2},{6,4},{8,6},{10,8},{12,10},{14,12},{16,14},{18,16},{20... | collective-permute-start | bytes 294920 | tf_op jit(solution)/shard_map/ppermute | solution.py:17
  70.4 26.9 %collective-permute-start.9 = (bf16[64,768]{1,0:T(8,128)(2,1)}, bf16[64,768]{1,0:T(8,128)(2,1)}, u32[]{:S(2)}, u32[]{:S(2)}) collective-permute-start(bf16[64,768]{1,0:T(8,128)(2,1)} %bitcast.23), channel_id=1, source_target_pairs={{0,2},{2,4},{4,6},{6,8},{8,10},{10,12},{12,14},{14,16},{16,18},{18... | collective-permute-start | bytes 294920 | tf_op jit(solution)/shard_map/ppermute | solution.py:17
  73.5 29.5 %collective-permute-start.8 = (bf16[64,768]{1,0:T(8,128)(2,1)}, bf16[64,768]{1,0:T(8,128)(2,1)}, u32[]{:S(2)}, u32[]{:S(2)}) collective-permute-start(bf16[64,768]{1,0:T(8,128)(2,1)} %bitcast.23), channel_id=1, source_target_pairs={{0,4},{2,6},{4,8},{6,10},{8,12},{10,14},{12,16},{14,18},{16,20},{1... | collective-permute-start | bytes 294920 | tf_op jit(solution)/shard_map/ppermute | solution.py:17
  79.0 49.4 %collective-permute-start.31 = (bf16[64,768]{1,0:T(8,128)(2,1)}, bf16[64,768]{1,0:T(8,128)(2,1)}, u32[]{:S(2)}, u32[]{:S(2)}) collective-permute-start(bf16[64,768]{1,0:T(8,128)(2,1)} %bitcast_multiply_fusion.1), channel_id=1, source_target_pairs={{4,0},{6,2},{8,4},{10,6},{12,8},{14,10},{16,12},{18,14},{20,16},{2... | collective-permute-start | bytes 294920 | tf_op jit(solution)/shard_map/ppermute | solution.py:17
  89.8 33.5 %collective-permute-start.30 = (bf16[64,768]{1,0:T(8,128)(2,1)}, bf16[64,768]{1,0:T(8,128)(2,1)}, u32[]{:S(2)}, u32[]{:S(2)}) collective-permute-start(bf16[64,768]{1,0:T(8,128)(2,1)} %bitcast_multiply_fusion.1), channel_id=1, source_target_pairs={{2,0},{4,2},{6,4},{8,6},{10,8},{12,10},{14,12},{16,14},{18,16},{20... | collective-permute-start | bytes 294920 | tf_op jit(solution)/shard_map/ppermute | solution.py:17
  94.2 24.0 %collective-permute-start.29 = (bf16[64,768]{1,0:T(8,128)(2,1)}, bf16[64,768]{1,0:T(8,128)(2,1)}, u32[]{:S(2)}, u32[]{:S(2)}) collective-permute-start(bf16[64,768]{1,0:T(8,128)(2,1)} %bitcast_multiply_fusion.1), channel_id=1, source_target_pairs={{0,2},{2,4},{4,6},{6,8},{8,10},{10,12},{12,14},{14,16},{16,18},{18... | collective-permute-start | bytes 294920 | tf_op jit(solution)/shard_map/ppermute | solution.py:17
  97.3 14.6 %collective-permute-start.28 = (bf16[64,768]{1,0:T(8,128)(2,1)}, bf16[64,768]{1,0:T(8,128)(2,1)}, u32[]{:S(2)}, u32[]{:S(2)}) collective-permute-start(bf16[64,768]{1,0:T(8,128)(2,1)} %bitcast_multiply_fusion.1), channel_id=1, source_target_pairs={{0,4},{2,6},{4,8},{6,10},{8,12},{10,14},{12,16},{14,18},{16,20},{1... | collective-permute-start | bytes 294920 | tf_op jit(solution)/shard_map/ppermute | solution.py:17
  110.0 20.9 %collective-permute-start.16 = (f32[12,64]{1,0:T(8,128)S(1)}, f32[12,64]{1,0:T(8,128)S(1)}, u32[]{:S(2)}, u32[]{:S(2)}) collective-permute-start(f32[12,64]{1,0:T(8,128)S(1)} %get-tuple-element.80), channel_id=1, source_target_pairs={{4,0},{6,2},{8,4},{10,6},{12,8},{14,10},{16,12},{18,14},{20,16},{2... | collective-permute-start | bytes 9224 | tf_op jit(solution)/shard_map/ppermute | solution.py:17
  111.9 23.3 %collective-permute-start.19 = (f32[12,64]{1,0:T(8,128)S(1)}, f32[12,64]{1,0:T(8,128)S(1)}, u32[]{:S(2)}, u32[]{:S(2)}) collective-permute-start(f32[12,64]{1,0:T(8,128)S(1)} %get-tuple-element.81), channel_id=1, source_target_pairs={{0,4},{2,6},{4,8},{6,10},{8,12},{10,14},{12,16},{14,18},{16,20},{1... | collective-permute-start | bytes 9224 | tf_op jit(solution)/shard_map/ppermute | solution.py:17
  118.3 18.9 %collective-permute-start.18 = (f32[12,64]{1,0:T(8,128)S(1)}, f32[12,64]{1,0:T(8,128)S(1)}, u32[]{:S(2)}, u32[]{:S(2)}) collective-permute-start(f32[12,64]{1,0:T(8,128)S(1)} %get-tuple-element.82), channel_id=1, source_target_pairs={{0,2},{2,4},{4,6},{6,8},{8,10},{10,12},{12,14},{14,16},{16,18},{18... | collective-permute-start | bytes 9224 | tf_op jit(solution)/shard_map/ppermute | solution.py:17
  123.3 31.2 %collective-permute-start.17 = (f32[12,64]{1,0:T(8,128)}, f32[12,64]{1,0:T(8,128)S(1)}, u32[]{:S(2)}, u32[]{:S(2)}) collective-permute-start(f32[12,64]{1,0:T(8,128)} %get-tuple-element.83), channel_id=1, source_target_pairs={{2,0},{4,2},{6,4},{8,6},{10,8},{12,10},{14,12},{16,14},{18,16},{20... | collective-permute-start | bytes 9224 | tf_op jit(solution)/shard_map/ppermute | solution.py:17
  128.4 27.9 %collective-permute-start.12 = (f32[12,64]{1,0:T(8,128)}, f32[12,64]{1,0:T(8,128)S(1)}, u32[]{:S(2)}, u32[]{:S(2)}) collective-permute-start(f32[12,64]{1,0:T(8,128)} %get-tuple-element.76), channel_id=1, source_target_pairs={{4,0},{6,2},{8,4},{10,6},{12,8},{14,10},{16,12},{18,14},{20,16},{2... | collective-permute-start | bytes 9224 | tf_op jit(solution)/shard_map/ppermute | solution.py:17
  130.9 25.5 %collective-permute-start.15 = (f32[12,64]{1,0:T(8,128)}, f32[12,64]{1,0:T(8,128)S(1)}, u32[]{:S(2)}, u32[]{:S(2)}) collective-permute-start(f32[12,64]{1,0:T(8,128)} %get-tuple-element.77), channel_id=1, source_target_pairs={{0,4},{2,6},{4,8},{6,10},{8,12},{10,14},{12,16},{14,18},{16,20},{1... | collective-permute-start | bytes 9224 | tf_op jit(solution)/shard_map/ppermute | solution.py:17
  135.2 21.2 %collective-permute-start.14 = (f32[12,64]{1,0:T(8,128)}, f32[12,64]{1,0:T(8,128)S(1)}, u32[]{:S(2)}, u32[]{:S(2)}) collective-permute-start(f32[12,64]{1,0:T(8,128)} %get-tuple-element.78), channel_id=1, source_target_pairs={{0,2},{2,4},{4,6},{6,8},{8,10},{10,12},{12,14},{14,16},{16,18},{18... | collective-permute-start | bytes 9224 | tf_op jit(solution)/shard_map/ppermute | solution.py:17
  137.2 19.3 %collective-permute-start.13 = (f32[12,64]{1,0:T(8,128)S(1)}, f32[12,64]{1,0:T(8,128)S(1)}, u32[]{:S(2)}, u32[]{:S(2)}) collective-permute-start(f32[12,64]{1,0:T(8,128)S(1)} %get-tuple-element.79), channel_id=1, source_target_pairs={{2,0},{4,2},{6,4},{8,6},{10,8},{12,10},{14,12},{16,14},{18,16},{20... | collective-permute-start | bytes 9224 | tf_op jit(solution)/shard_map/ppermute | solution.py:17
  154.5 38.0 %collective-permute-start.41 = (f32[64,768]{1,0:T(8,128)}, f32[64,768]{1,0:T(8,128)}, u32[]{:S(2)}, u32[]{:S(2)}) collective-permute-start(f32[64,768]{1,0:T(8,128)} %copy.290), channel_id=1, source_target_pairs={{2,0},{4,2},{6,4},{8,6},{10,8},{12,10},{14,12},{16,14},{18,16},{20... | collective-permute-start | bytes 589832 | tf_op jit(solution)/shard_map/ppermute | solution.py:17
  156.5 17.8 %collective-permute-start.23 = (f32[12,64]{1,0:T(8,128)S(1)}, f32[12,64]{1,0:T(8,128)S(1)}, u32[]{:S(2)}, u32[]{:S(2)}) collective-permute-start(f32[12,64]{1,0:T(8,128)S(1)} %fusion.17), channel_id=1, source_target_pairs={{4,0},{6,2},{8,4},{10,6},{12,8},{14,10},{16,12},{18,14},{20,16},{2... | collective-permute-start | bytes 9224 | tf_op jit(solution)/shard_map/ppermute | solution.py:17
  159.3 18.0 %collective-permute-start.22 = (f32[12,64]{1,0:T(8,128)S(1)}, f32[12,64]{1,0:T(8,128)S(1)}, u32[]{:S(2)}, u32[]{:S(2)}) collective-permute-start(f32[12,64]{1,0:T(8,128)S(1)} %fusion.17), channel_id=1, source_target_pairs={{2,0},{4,2},{6,4},{8,6},{10,8},{12,10},{14,12},{16,14},{18,16},{20... | collective-permute-start | bytes 9224 | tf_op jit(solution)/shard_map/ppermute | solution.py:17
  162.7 17.9 %collective-permute-start.21 = (f32[12,64]{1,0:T(8,128)S(1)}, f32[12,64]{1,0:T(8,128)S(1)}, u32[]{:S(2)}, u32[]{:S(2)}) collective-permute-start(f32[12,64]{1,0:T(8,128)S(1)} %fusion.17), channel_id=1, source_target_pairs={{0,2},{2,4},{4,6},{6,8},{8,10},{10,12},{12,14},{14,16},{16,18},{18... | collective-permute-start | bytes 9224 | tf_op jit(solution)/shard_map/ppermute | solution.py:17
  164.6 18.6 %collective-permute-start.20 = (f32[12,64]{1,0:T(8,128)S(1)}, f32[12,64]{1,0:T(8,128)S(1)}, u32[]{:S(2)}, u32[]{:S(2)}) collective-permute-start(f32[12,64]{1,0:T(8,128)S(1)} %fusion.17), channel_id=1, source_target_pairs={{0,4},{2,6},{4,8},{6,10},{8,12},{10,14},{12,16},{14,18},{16,20},{1... | collective-permute-start | bytes 9224 | tf_op jit(solution)/shard_map/ppermute | solution.py:17
  174.2 20.8 %collective-permute-start.42 = (f32[64,768]{1,0:T(8,128)}, f32[64,768]{1,0:T(8,128)}, u32[]{:S(2)}, u32[]{:S(2)}) collective-permute-start(f32[64,768]{1,0:T(8,128)} %copy.291), channel_id=1, source_target_pairs={{0,2},{2,4},{4,6},{6,8},{8,10},{10,12},{12,14},{14,16},{16,18},{18... | collective-permute-start | bytes 589832 | tf_op jit(solution)/shard_map/ppermute | solution.py:17
  177.3 19.6 %collective-permute-start.43 = (f32[64,768]{1,0:T(8,128)}, f32[64,768]{1,0:T(8,128)}, u32[]{:S(2)}, u32[]{:S(2)}) collective-permute-start(f32[64,768]{1,0:T(8,128)} %copy.292), channel_id=1, source_target_pairs={{0,4},{2,6},{4,8},{6,10},{8,12},{10,14},{12,16},{14,18},{16,20},{1... | collective-permute-start | bytes 589832 | tf_op jit(solution)/shard_map/ppermute | solution.py:17
  180.6 19.8 %collective-permute-start.40 = (f32[64,768]{1,0:T(8,128)}, f32[64,768]{1,0:T(8,128)}, u32[]{:S(2)}, u32[]{:S(2)}) collective-permute-start(f32[64,768]{1,0:T(8,128)} %copy.288), channel_id=1, source_target_pairs={{4,0},{6,2},{8,4},{10,6},{12,8},{14,10},{16,12},{18,14},{20,16},{2... | collective-permute-start | bytes 589832 | tf_op jit(solution)/shard_map/ppermute | solution.py:17
  183.8 40.4 %collective-permute-start.45 = (f32[64,768]{1,0:T(8,128)}, f32[64,768]{1,0:T(8,128)}, u32[]{:S(2)}, u32[]{:S(2)}) collective-permute-start(f32[64,768]{1,0:T(8,128)} %copy.296), channel_id=1, source_target_pairs={{2,0},{4,2},{6,4},{8,6},{10,8},{12,10},{14,12},{16,14},{18,16},{20... | collective-permute-start | bytes 589832 | tf_op jit(solution)/shard_map/ppermute | solution.py:17
  192.5 16.3 %collective-permute-start.25 = (f32[64,768]{1,0:T(8,128)S(1)}, f32[64,768]{1,0:T(8,128)S(1)}, u32[]{:S(2)}, u32[]{:S(2)}) collective-permute-start(f32[64,768]{1,0:T(8,128)S(1)} %copy.270), channel_id=1, source_target_pairs={{2,0},{4,2},{6,4},{8,6},{10,8},{12,10},{14,12},{16,14},{18,16},{20... | collective-permute-start | bytes 589832 | tf_op jit(solution)/shard_map/ppermute | solution.py:17
  195.0 16.7 %collective-permute-start.26 = (f32[64,768]{1,0:T(8,128)S(1)}, f32[64,768]{1,0:T(8,128)S(1)}, u32[]{:S(2)}, u32[]{:S(2)}) collective-permute-start(f32[64,768]{1,0:T(8,128)S(1)} %copy.271), channel_id=1, source_target_pairs={{0,2},{2,4},{4,6},{6,8},{8,10},{10,12},{12,14},{14,16},{16,18},{18... | collective-permute-start | bytes 589832 | tf_op jit(solution)/shard_map/ppermute | solution.py:17
  197.0 18.9 %collective-permute-start.27 = (f32[64,768]{1,0:T(8,128)S(1)}, f32[64,768]{1,0:T(8,128)S(1)}, u32[]{:S(2)}, u32[]{:S(2)}) collective-permute-start(f32[64,768]{1,0:T(8,128)S(1)} %copy.272), channel_id=1, source_target_pairs={{0,4},{2,6},{4,8},{6,10},{8,12},{10,14},{12,16},{14,18},{16,20},{1... | collective-permute-start | bytes 589832 | tf_op jit(solution)/shard_map/ppermute | solution.py:17
  200.4 17.4 %collective-permute-start.24 = (f32[64,768]{1,0:T(8,128)}, f32[64,768]{1,0:T(8,128)S(1)}, u32[]{:S(2)}, u32[]{:S(2)}) collective-permute-start(f32[64,768]{1,0:T(8,128)} %copy.268), channel_id=1, source_target_pairs={{4,0},{6,2},{8,4},{10,6},{12,8},{14,10},{16,12},{18,14},{20,16},{2... | collective-permute-start | bytes 589832 | tf_op jit(solution)/shard_map/ppermute | solution.py:17
  204.8 53.9 %all-to-all-start.6 = ((bf16[2,32,768]{2,1,0:T(8,128)(2,1)}), bf16[2,32,768]{2,1,0:T(8,128)(2,1)}, u32[]{:S(2)}, u32[]{:S(2)}) async-start(bf16[2,32,768]{2,1,0:T(8,128)(2,1)} %bitcast.67), calls=%async_computation.6 | async-start | bytes 196608 | tf_op jit(solution)/shard_map/all_to_all | solution.py:232
  208.8 18.2 %collective-permute-start.46 = (f32[64,768]{1,0:T(8,128)}, f32[64,768]{1,0:T(8,128)S(1)}, u32[]{:S(2)}, u32[]{:S(2)}) collective-permute-start(f32[64,768]{1,0:T(8,128)} %copy.297), channel_id=1, source_target_pairs={{0,2},{2,4},{4,6},{6,8},{8,10},{10,12},{12,14},{14,16},{16,18},{18... | collective-permute-start | bytes 589832 | tf_op jit(solution)/shard_map/ppermute | solution.py:17
  211.7 17.2 %collective-permute-start.47 = (f32[64,768]{1,0:T(8,128)}, f32[64,768]{1,0:T(8,128)S(1)}, u32[]{:S(2)}, u32[]{:S(2)}) collective-permute-start(f32[64,768]{1,0:T(8,128)} %copy.298), channel_id=1, source_target_pairs={{0,4},{2,6},{4,8},{6,10},{8,12},{10,14},{12,16},{14,18},{16,20},{1... | collective-permute-start | bytes 589832 | tf_op jit(solution)/shard_map/ppermute | solution.py:17
  215.9 16.2 %collective-permute-start.44 = (f32[64,768]{1,0:T(8,128)}, f32[64,768]{1,0:T(8,128)S(1)}, u32[]{:S(2)}, u32[]{:S(2)}) collective-permute-start(f32[64,768]{1,0:T(8,128)} %copy.294), channel_id=1, source_target_pairs={{4,0},{6,2},{8,4},{10,6},{12,8},{14,10},{16,12},{18,14},{20,16},{2... | collective-permute-start | bytes 589832 | tf_op jit(solution)/shard_map/ppermute | solution.py:17
  219.9 13.9 %collective-permute-start.35 = (f32[64,12]{1,0:T(8,128)S(1)}, f32[64,12]{1,0:T(8,128)S(1)}, u32[]{:S(2)}, u32[]{:S(2)}) collective-permute-start(f32[64,12]{1,0:T(8,128)S(1)} %multiply_reduce_fusion.1), channel_id=1, source_target_pairs={{4,0},{6,2},{8,4},{10,6},{12,8},{14,10},{16,12},{18,14},{20,16},{2... | collective-permute-start | bytes 9224 | tf_op jit(solution)/shard_map/ppermute | solution.py:17
  224.2 9.7 %collective-permute-start.34 = (f32[64,12]{1,0:T(8,128)S(1)}, f32[64,12]{1,0:T(8,128)S(1)}, u32[]{:S(2)}, u32[]{:S(2)}) collective-permute-start(f32[64,12]{1,0:T(8,128)S(1)} %multiply_reduce_fusion.1), channel_id=1, source_target_pairs={{2,0},{4,2},{6,4},{8,6},{10,8},{12,10},{14,12},{16,14},{18,16},{20... | collective-permute-start | bytes 9224 | tf_op jit(solution)/shard_map/ppermute | solution.py:17
  247.3 23.6 %collective-permute-start.37 = (f32[64,768]{1,0:T(8,128)}, f32[64,768]{1,0:T(8,128)}, u32[]{:S(2)}, u32[]{:S(2)}) collective-permute-start(f32[64,768]{1,0:T(8,128)} %copy.284), channel_id=1, source_target_pairs={{2,0},{4,2},{6,4},{8,6},{10,8},{12,10},{14,12},{16,14},{18,16},{20... | collective-permute-start | bytes 589832 | tf_op jit(solution)/shard_map/ppermute | solution.py:17
  250.7 20.2 %collective-permute-start.38 = (f32[64,768]{1,0:T(8,128)}, f32[64,768]{1,0:T(8,128)}, u32[]{:S(2)}, u32[]{:S(2)}) collective-permute-start(f32[64,768]{1,0:T(8,128)} %copy.285), channel_id=1, source_target_pairs={{0,2},{2,4},{4,6},{6,8},{8,10},{10,12},{12,14},{14,16},{16,18},{18... | collective-permute-start | bytes 589832 | tf_op jit(solution)/shard_map/ppermute | solution.py:17
  252.8 18.1 %collective-permute-start.39 = (f32[64,768]{1,0:T(8,128)}, f32[64,768]{1,0:T(8,128)}, u32[]{:S(2)}, u32[]{:S(2)}) collective-permute-start(f32[64,768]{1,0:T(8,128)} %copy.286), channel_id=1, source_target_pairs={{0,4},{2,6},{4,8},{6,10},{8,12},{10,14},{12,16},{14,18},{16,20},{1... | collective-permute-start | bytes 589832 | tf_op jit(solution)/shard_map/ppermute | solution.py:17
  255.9 15.0 %collective-permute-start.36 = (f32[64,768]{1,0:T(8,128)}, f32[64,768]{1,0:T(8,128)}, u32[]{:S(2)}, u32[]{:S(2)}) collective-permute-start(f32[64,768]{1,0:T(8,128)} %copy.282), channel_id=1, source_target_pairs={{4,0},{6,2},{8,4},{10,6},{12,8},{14,10},{16,12},{18,14},{20,16},{2... | collective-permute-start | bytes 589832 | tf_op jit(solution)/shard_map/ppermute | solution.py:17
  (19 other events, 259.2 us)
where the time goes:
time: 290 us; the launch traced here: 284 us
  starting transfers between devices  166 us (57%)
  local copies, waits for them, and re-layouts  72.8 us (25%)
  matrix products  23 us (8%)
  other arithmetic  12.8 us (4%)
  waiting for transfers between devices  8.36 us (3%)
    ppermute x48, starting transfers between devices, from_behind(): lax.ppermute(value, axis, [(source, source + steps) for source in range(l...  137 us
    slice x26, local copies, waits for them, and re-layouts, rows_of(): lax.slice_in_dim(tensor, (window_shift + reach_dev) * size, (window_shift...  25.9 us
    unnamed x34, local copies, waits for them, and re-layouts  17 us
    concatenate x13, local copies, waits for them, and re-layouts, nearby_row_span(): jnp.concatenate([pieces[window_shift] for window_shift in range(-reach_de...  8.03 us
    ppermute x16, local copies, waits for them, and re-layouts, from_behind(): lax.ppermute(value, axis, [(source, source + steps) for source in range(l...  7.63 us
  transfers between devices with their start and end apart: 56, of which 6 were waited for; matrix products, arithmetic and copies ran while one was open for 36% of the time, Pallas kernels for 0%

commit v1 on v0

v1 whole, which is shorter than its diff:
```python
import functools

import jax
import jax.numpy as jnp
from jax import lax
from jax.experimental import pallas as pl
from jax.experimental.pallas import tpu as pltpu
from jax.sharding import PartitionSpec as P

HD = 64
BLK = 64
WMAX = 3
NEG = -1e30
FLOOR = -1e29
REACH = WMAX - 1
SLOTS = 2 * REACH + 1
OWN = REACH
PAIR = 2 * HD

F32 = jnp.float32
BF16 = jnp.bfloat16


def dot_nt(a, b):
    return lax.dot_general(a, b, (((1,), (1,)), ((), ())), preferred_element_type=F32)


def dot_nn(a, b):
    return lax.dot_general(a, b, (((1,), (0,)), ((), ())), preferred_element_type=F32)


def dot_tn(a, b):
    return lax.dot_general(a, b, (((0,), (0,)), ((), ())), preferred_element_type=F32)


def kernel(
    n,
    win,
    alen,
    qv,
    kv,
    vv,
    gv,
    qa,
    ka,
    va,
    ga,
    out_v,
    out_a,
    dq_v,
    dk_v,
    dv_v,
    dq_a,
    dk_a,
    dv_a,
    near,
    e_buf,
    dp_buf,
    bias_va,
    bias_av,
    vmask,
    stats,
    stats_in,
    res,
    part,
    sendb,
    mate_in,
    far_in,
    fin,
    x_send,
    x_recv,
    far_send,
    far_recv,
    mate_send,
    mate_recv,
    relay_send,
    relay_recv,
    st_send,
    st_recv,
    rs_send,
    rs_recv,
    rm_send,
    rm_recv,
    rf_send,
    rf_recv,
    xo_send,
    xo_recv,
):
    d = lax.axis_index("vid")
    a = lax.axis_index("aud")
    odd = lax.rem(d, 2)
    mate = d + 1 - 2 * odd
    peer = 1 - a
    half = qa.shape[0]
    width = qv.shape[1]
    vrows = qv.shape[0]
    arows = 2 * half
    vblocks = vrows // BLK
    heads = width // HD
    pairs = width // PAIR
    has = {o: (d + o >= 0) & (d + o < n) for o in (-2, -1, 1, 2)}

    def at(vid):
        return {"vid": vid, "aud": a}

    def remote(src, dst, s, r, dev):
        return pltpu.make_async_remote_copy(
            src_ref=src,
            dst_ref=dst,
            send_sem=s,
            recv_sem=r,
            device_id=dev,
            device_id_type=pl.DeviceIdType.MESH,
        )

    def rows(slot, t, size):
        return pl.ds(pl.multiple_of(slot * arows + t * half, half), size)

    barrier = pltpu.get_barrier_semaphore()
    pl.semaphore_signal(
        barrier, inc=1, device_id={"vid": d, "aud": peer}, device_id_type=pl.DeviceIdType.MESH
    )
    for o in has:

        @pl.when(has[o])
        def _(o=o):
            pl.semaphore_signal(
                barrier, inc=1, device_id=at(d + o), device_id_type=pl.DeviceIdType.MESH
            )

    ins = (qa, ga, ka, va)
    own_cols = pl.ds(pl.multiple_of(a * width, width), width)
    peer_cols = pl.ds(pl.multiple_of(peer * width, width), width)
    for t in range(4):
        near[t, rows(OWN, a, half), :] = ins[t][:, own_cols]

    pl.semaphore_wait(barrier, 1 + sum(jnp.where(has[o], 1, 0) for o in has))

    x_copy = [
        remote(
            ins[t].at[:, peer_cols],
            near.at[t, rows(OWN, a, half)],
            x_send.at[t],
            x_recv.at[t],
            {"vid": d, "aud": peer},
        )
        for t in range(4)
    ]

    def x_arrived(t):
        return remote(
            ins[t].at[:, own_cols],
            near.at[t, rows(OWN, peer, half)],
            x_send.at[t],
            x_recv.at[t],
            {"vid": d, "aud": peer},
        )

    def piece(group, slot, which):
        return near.at[pl.ds(2 * group, 2), rows(slot, a if which == 0 else peer, half)]

    def far_copy(group, which, side):
        o = (-2, 2)[side]
        return remote(
            piece(group, OWN, which),
            piece(group, OWN - o, which),
            far_send.at[group, which, side],
            far_recv.at[group, which, 1 - side],
            at(d + o),
        )

    def far_arrived(group, which, side):
        o = (-2, 2)[side]
        return remote(
            piece(group, OWN, which),
            piece(group, OWN + o, which),
            far_send.at[group, which, side],
            far_recv.at[group, which, side],
            at(d + o),
        )

    def mate_copy(group, which, slot):
        return remote(
            piece(group, OWN, which),
            piece(group, slot, which),
            mate_send.at[group, which],
            mate_recv.at[group, which],
            at(mate),
        )

    def relay_copy(group, which, src_slot, slot):
        return remote(
            piece(group, src_slot, which),
            piece(group, slot, which),
            relay_send.at[group, which],
            relay_recv.at[group, which],
            at(mate),
        )

    low_slot = 1 + 2 * odd
    high_slot = 3 - 2 * odd
    relay_from = 4 - 4 * odd
    relays_out = ((odd == 0) & has[2]) | ((odd == 1) & has[-2])
    relays_in = ((odd == 0) & has[-1]) | ((odd == 1) & has[1])

    def send_own(group, which):
        for side in range(2):

            @pl.when(has[(-2, 2)[side]])
            def _(side=side):
                far_copy(group, which, side).start()

        mate_copy(group, which, low_slot).start()

    def take_and_relay(group, which):
        for side in range(2):

            @pl.when(has[(-2, 2)[side]])
            def _(side=side):
                far_arrived(group, which, side).wait_recv()

        @pl.when(relays_out)
        def _():
            relay_copy(group, which, relay_from, low_slot + 2 * (1 - 2 * odd)).start()

    def finish_group(group):
        for which in range(2):
            mate_copy(group, which, high_slot).wait_recv()

            @pl.when(relays_in)
            def _(which=which):
                relay_copy(group, which, relay_from, low_slot).wait_recv()

    x_copy[0].start()
    x_copy[1].start()
    send_own(0, 0)
    x_copy[2].start()
    x_copy[3].start()

    for slot in range(SLOTS):
        o = slot - OWN
        if o != 0:

            @pl.when(jnp.logical_not(has[o]))
            def _(slot=slot):
                span = pl.ds(slot * arows, arows)
                near[:, span, :] = jnp.zeros((4, arows, width), BF16)
                stats_in[span, :] = jnp.full((arows, 128), NEG, F32)
                res[span, :] = jnp.zeros((arows, 128), F32)

    for side in range(2):

        @pl.when(jnp.logical_not(has[(-2, 2)[side]]))
        def _(side=side):
            far_in[:, side] = jnp.zeros((2, 2, arows, width), BF16)

    vb = lax.broadcasted_iota(jnp.int32, (arows, vrows), 1) // BLK
    tok = lax.broadcasted_iota(jnp.int32, (arows, vrows), 0)
    tok_l = lax.broadcasted_iota(jnp.int32, (arows, PAIR), 0)
    lens = []
    for slot in range(SLOTS):
        ablk = d + (slot - OWN)
        length = alen[lax.rem(ablk + n, n)]
        lens.append(length)
        bias = jnp.full((arows, vrows), NEG, F32)
        for b in range(vblocks):
            first = win[d * vblocks + b, 0]
            number = win[d * vblocks + b, 1]
            ok = (ablk >= first) & (ablk < first + number)
            bias = jnp.where(vb == b, jnp.where(ok, 0.0, NEG), bias)
        span = pl.ds(slot * arows, arows)
        bias_av[span, :] = bias
        bias_va[span, :] = jnp.where(tok < length, bias, NEG)
        vmask[span, :] = jnp.where(tok_l < length, 1.0, 0.0).astype(BF16)

    lane_w = lax.broadcasted_iota(jnp.int32, (1, PAIR), 1)
    half_mask = [
        jnp.where((lane_w >= HD * h) & (lane_w < HD * (h + 1)), 1.0, 0.0).astype(BF16)
        for h in range(2)
    ]
    lane_s = lax.broadcasted_iota(jnp.int32, (SLOTS * arows, 128), 1)
    stats[...] = jnp.zeros_like(stats)

    def both(low, high):
        lane = lax.broadcasted_iota(jnp.int32, low.shape, 1)
        return jnp.where(lane < HD, low, high)

    x_arrived(0).wait_recv()
    x_arrived(1).wait_recv()
    send_own(0, 1)
    send_own(1, 0)
    take_and_relay(0, 0)
    x_arrived(2).wait_recv()
    x_arrived(3).wait_recv()
    send_own(1, 1)
    take_and_relay(0, 1)
    finish_group(0)

    scale = HD**-0.5

    def cols(i):
        return pl.ds(pl.multiple_of(i * PAIR, PAIR), PAIR)

    def av_scores(i, carry):
        c = cols(i)
        q = near[0, :, c] * jnp.asarray(scale, BF16)
        g = near[1, :, c] * vmask[...]
        k = kv[:, c]
        v = vv[:, c]
        for h in range(2):
            s = dot_nt(q * half_mask[h], k) + bias_av[...]
            dp = dot_nt(g * half_mask[h], v)
            m = jnp.maximum(jnp.max(s, axis=1, keepdims=True), FLOOR)
            e = jnp.exp(s - m)
            total = jnp.sum(e, axis=1, keepdims=True)
            mixed = jnp.sum(e * dp, axis=1, keepdims=True)
            e_buf[2 * i + h] = e
            dp_buf[2 * i + h] = dp
            head = 2 * i + h
            old = stats[...]
            old = jnp.where(lane_s == head, m, old)
            old = jnp.where(lane_s == head + heads, total, old)
            stats[...] = jnp.where(lane_s == head + 2 * heads, mixed, old)
        return carry

    lax.fori_loop(0, pairs, av_scores, 0)

    def stats_copy(o):
        src = pl.ds((OWN + o) * arows, arows)
        dst = pl.ds((OWN - o) * arows, arows)
        return remote(
            stats.at[src], stats_in.at[dst], st_send.at[OWN + o], st_recv.at[OWN - o], at(d + o)
        )

    def stats_arrived(o):
        span = pl.ds((OWN + o) * arows, arows)
        return remote(
            stats.at[span], stats_in.at[span], st_send.at[OWN + o], st_recv.at[OWN + o], at(d + o)
        )

    def res_copy(o):
        return remote(
            res.at[pl.ds(OWN * arows, arows)],
            res.at[pl.ds((OWN - o) * arows, arows)],
            rs_send.at[OWN + o],
            rs_recv.at[OWN - o],
            at(d + o),
        )

    def res_arrived(o):
        return remote(
            res.at[pl.ds(OWN * arows, arows)],
            res.at[pl.ds((OWN + o) * arows, arows)],
            rs_send.at[OWN + o],
            rs_recv.at[OWN + o],
            at(d + o),
        )

    def each(make, action):
        for o in has:

            @pl.when(has[o])
            def _(o=o):
                action(make(o))

    each(stats_copy, lambda c: c.start())
    own_span = pl.ds(OWN * arows, arows)
    stats_in[own_span, :] = stats[own_span, :]

    take_and_relay(1, 0)
    take_and_relay(1, 1)
    finish_group(1)

    def store_part(kind, member, c, value):
        part[kind, member, :, c] = value
        sendb[kind, member, :, c] = value.astype(BF16)

    def va_all(i, carry):
        c = cols(i)
        k = near[2, :, c]
        v = near[3, :, c]
        q = qv[:, c] * jnp.asarray(scale, BF16)
        g = gv[:, c]
        o, dq, dk, dv = [], [], [], []
        for h in range(2):
            s = dot_nt(k * half_mask[h], q) + bias_va[...]
            dp = dot_nt(v * half_mask[h], g)
            m = jnp.max(s, axis=0, keepdims=True)
            e = jnp.exp(s - m)
            p = e * (1.0 / jnp.sum(e, axis=0, keepdims=True))
            delta = jnp.sum(p * dp, axis=0, keepdims=True)
            pb = p.astype(BF16)
            ds = (p * (dp - delta)).astype(BF16)
            o.append(dot_tn(pb, v))
            dq.append(dot_tn(ds, k))
            dk.append(dot_nn(ds, q))
            dv.append(dot_nn(pb, g))
        out_v[:, c] = both(*o).astype(BF16)
        dq_v[:, c] = (both(*dq) * scale).astype(BF16)
        store_part(0, 0, c, both(*dk))
        store_part(0, 1, c, both(*dv))
        return carry

    lax.fori_loop(0, pairs // 2, va_all, 0)

    each(stats_arrived, lambda c: c.wait_recv())
    parts = [stats_in[pl.ds(slot * arows, arows), :] for slot in range(SLOTS)]
    top = functools.reduce(jnp.maximum, parts)
    total = jnp.zeros_like(top)
    mixed = jnp.zeros_like(top)
    for x in parts:
        weight = jnp.exp(x - top)
        total = total + weight * pltpu.roll(x, 128 - heads, 1)
        mixed = mixed + weight * pltpu.roll(x, 128 - 2 * heads, 1)
    lane_o = lax.broadcasted_iota(jnp.int32, top.shape, 1)
    res[own_span, :] = jnp.where(
        lane_o < heads, top + jnp.log(total), pltpu.roll(mixed / total, heads, 1)
    )
    each(res_copy, lambda c: c.start())

    lax.fori_loop(pairs // 2, pairs, va_all, 0)

    def rm_copy(kind, to_owner, src_slot):
        span = pl.ds(pl.multiple_of(src_slot * arows, arows), arows)
        return remote(
            sendb.at[kind, :, span],
            mate_in.at[kind, to_owner],
            rm_send.at[kind, to_owner],
            rm_recv.at[kind, to_owner],
            at(mate),
        )

    def rf_copy(kind, side):
        slot = (0, 4)[side]
        return remote(
            sendb.at[kind, :, pl.ds(slot * arows, arows)],
            far_in.at[kind, 1 - side],
            rf_send.at[kind, side],
            rf_recv.at[kind, 1 - side],
            at(d + (-2, 2)[side]),
        )

    def rf_arrived(kind, side):
        return remote(
            sendb.at[kind, :, pl.ds(0, arows)],
            far_in.at[kind, side],
            rf_send.at[kind, side],
            rf_recv.at[kind, side],
            at(d + (-2, 2)[side]),
        )

    def return_first(kind):
        @pl.when(relays_in)
        def _():
            rm_copy(kind, 0, low_slot).start()

        @pl.when((odd == 0) & has[-2])
        def _():
            rf_copy(kind, 0).start()

        @pl.when((odd == 1) & has[2])
        def _():
            rf_copy(kind, 1).start()

        rm_copy(kind, 1, high_slot).start()

    def return_second(kind):
        for side, parity in ((1, 0), (0, 1)):

            @pl.when((odd == parity) & has[(-2, 2)[side]])
            def _(side=side):
                rm_copy(kind, 0, low_slot).wait_recv()
                span = pl.ds((0, 4)[side] * arows, arows)
                for member in range(2):
                    sendb[kind, member, span, :] = (
                        part[kind, member, span, :] + mate_in[kind, 0, member].astype(F32)
                    ).astype(BF16)
                rf_copy(kind, side).start()

    finals = ((dk_a, dv_a), (out_a, dq_a))

    def xo_copy(kind, member):
        return remote(
            fin.at[kind, member, pl.ds(pl.multiple_of(peer * half, half), half)],
            finals[kind][member].at[:, own_cols],
            xo_send.at[kind, member],
            xo_recv.at[kind, member],
            {"vid": d, "aud": peer},
        )

    def xo_arrived(kind, member):
        return remote(
            fin.at[kind, member, pl.ds(pl.multiple_of(peer * half, half), half)],
            finals[kind][member].at[:, peer_cols],
            xo_send.at[kind, member],
            xo_recv.at[kind, member],
            {"vid": d, "aud": peer},
        )

    def return_last(kind):
        rm_copy(kind, 1, high_slot).wait_recv()
        for side in range(2):

            @pl.when(has[(-2, 2)[side]])
            def _(side=side):
                rf_arrived(kind, side).wait_recv()

        for member in range(2):
            value = (
                part[kind, member, own_span, :]
                + mate_in[kind, 1, member].astype(F32)
                + far_in[kind, 0, member].astype(F32)
                + far_in[kind, 1, member].astype(F32)
            )
            if kind == 1 and member == 0:
                token = lax.broadcasted_iota(jnp.int32, value.shape, 0)
                value = jnp.where(token < lens[OWN], value, 0.0)
            fin[kind, member] = value.astype(BF16)
            xo_copy(kind, member).start()
            finals[kind][member][:, own_cols] = fin[
                kind, member, pl.ds(pl.multiple_of(a * half, half), half), :
            ]

    return_first(0)
    each(res_arrived, lambda c: c.wait_recv())

    def av_all(i, carry):
        c = cols(i)
        q = near[0, :, c] * jnp.asarray(scale, BF16)
        g = near[1, :, c] * vmask[...]
        k = kv[:, c]
        v = vv[:, c]
        o, dq, dk, dv = [], [], [], []
        lane = lax.broadcasted_iota(jnp.int32, (SLOTS * arows, 128), 1)
        for h in range(2):
            head = 2 * i + h
            gap = jnp.sum(jnp.where(lane == head, stats[...] - res[...], 0.0), 1, keepdims=True)
            delta = jnp.sum(jnp.where(lane == head + heads, res[...], 0.0), 1, keepdims=True)
            p = e_buf[head] * jnp.exp(gap)
            pb = p.astype(BF16)
            ds = (p * (dp_buf[head] - delta)).astype(BF16)
            o.append(dot_nn(pb, v))
            dq.append(dot_nn(ds, k))
            dk.append(dot_tn(ds, q))
            dv.append(dot_tn(pb, g))
        store_part(1, 0, c, both(*o))
        store_part(1, 1, c, both(*dq) * scale)
        dk_v[:, c] = both(*dk).astype(BF16)
        dv_v[:, c] = both(*dv).astype(BF16)
        return carry

    lax.fori_loop(0, pairs // 2, av_all, 0)
    return_second(0)
    lax.fori_loop(pairs // 2, pairs, av_all, 0)
    return_first(1)
    return_second(1)
    return_last(0)
    return_last(1)
    for kind in range(2):
        for member in range(2):
            xo_arrived(kind, member).wait_recv()

    for t in range(4):
        x_copy[t].wait_send()
    for group in range(2):
        for which in range(2):
            for side in range(2):

                @pl.when(has[(-2, 2)[side]])
                def _(group=group, which=which, side=side):
                    far_copy(group, which, side).wait_send()

            mate_copy(group, which, low_slot).wait_send()

            @pl.when(relays_out)
            def _(group=group, which=which):
                relay_copy(group, which, relay_from, high_slot).wait_send()

    each(stats_copy, lambda c: c.wait_send())
    each(res_copy, lambda c: c.wait_send())
    for kind in range(2):

        @pl.when(relays_in)
        def _(kind=kind):
            rm_copy(kind, 0, low_slot).wait_send()

        rm_copy(kind, 1, high_slot).wait_send()
        for side in range(2):

            @pl.when(has[(-2, 2)[side]])
            def _(kind=kind, side=side):
                rf_copy(kind, side).wait_send()

        for member in range(2):
            xo_copy(kind, member).wait_send()


def body(n, q_video, k_video, v_video, g_video, q_audio, k_audio, v_audio, g_audio, window, alen):
    vrows, width = q_video.shape
    half, full = q_audio.shape
    arows = 2 * half
    heads = width // HD
    near_rows = SLOTS * arows
    assert arows == BLK and n % 2 == 0 and 3 * heads <= 128 and width % (2 * PAIR) == 0
    video = jax.ShapeDtypeStruct((vrows, width), BF16)
    audio = jax.ShapeDtypeStruct((half, full), BF16)
    dma = pltpu.SemaphoreType.DMA
    vmem = pl.BlockSpec(memory_space=pltpu.VMEM)
    smem = pl.BlockSpec(memory_space=pltpu.SMEM)
    sems = [(4,), (2, 2, 2), (2, 2), (2, 2), (SLOTS,), (SLOTS,), (2, 2), (2, 2), (2, 2)]
    return pl.pallas_call(
        functools.partial(kernel, n),
        out_shape=(video, audio, video, video, video, audio, audio, audio),
        in_specs=[smem] * 2 + [vmem] * 8,
        out_specs=(vmem,) * 8,
        scratch_shapes=[
            pltpu.VMEM((4, near_rows, width), BF16),
            pltpu.VMEM((heads, near_rows, vrows), F32),
            pltpu.VMEM((heads, near_rows, vrows), F32),
            pltpu.VMEM((near_rows, vrows), F32),
            pltpu.VMEM((near_rows, vrows), F32),
            pltpu.VMEM((near_rows, PAIR), BF16),
            pltpu.VMEM((near_rows, 128), F32),
            pltpu.VMEM((near_rows, 128), F32),
            pltpu.VMEM((near_rows, 128), F32),
            pltpu.VMEM((2, 2, near_rows, width), F32),
            pltpu.VMEM((2, 2, near_rows, width), BF16),
            pltpu.VMEM((2, 2, 2, arows, width), BF16),
            pltpu.VMEM((2, 2, 2, arows, width), BF16),
            pltpu.VMEM((2, 2, arows, width), BF16),
        ]
        + [dma(shape) for shape in sems for _ in range(2)],
        compiler_params=pltpu.CompilerParams(
            collective_id=0, has_side_effects=True, vmem_limit_bytes=48 * 1024 * 1024
        ),
    )(window, alen, q_video, k_video, v_video, g_video, q_audio, k_audio, v_audio, g_audio)


def solution(mesh):
    tokens = P("vid", "aud")
    stretch = P(("vid", "aud"), None)
    return jax.shard_map(
        functools.partial(body, mesh.shape["vid"]),
        mesh=mesh,
        in_specs=(tokens,) * 4 + (stretch,) * 4 + (P(), P()),
        out_specs=(tokens, stretch, tokens, tokens, tokens, stretch, stretch, stretch),
        check_vma=False,
    )
```

time: 290 us -> 70.5 us (0.24); the launches traced: 284 us -> 70.1 us
  starting transfers between devices: 166 us -> 0 us
  local copies, waits for them, and re-layouts: 72.8 us -> 13.9 us
  Pallas kernels: 0 us -> 55.5 us
  matrix products: 23 us -> 0 us
  other arithmetic: 12.8 us -> 0 us
  waiting for transfers between devices: 8.36 us -> 0 us
    ppermute x48 -> x0, starting transfers between devices: 137 us -> none  [from_behind(): lax.ppermute(value, axis, [(source, source + steps) for source in range(l...]
    pallas_call x0 -> x1, Pallas kernels: none -> 55.5 us  [body(): pl.pallas_call(functools.partial(kernel, n), out_shape=(video, audio, vid...]
    all_to_all x8 -> x0, starting transfers between devices: 28.6 us -> none  [the longest x1 3.97 us: body(): lax.all_to_all(dv_aud.astype(jnp.bfloat16), 'aud', split_axis=0, concat_a...]
    slice x26 -> x0, local copies, waits for them, and re-layouts: 25.9 us -> none  [rows_of(): lax.slice_in_dim(tensor, (window_shift + reach_dev) * size, (window_shift...]
    dot_general x12 -> x0, matrix products: 23 us -> none  [the longest x2 5.66 us: gradient_terms(): jnp.einsum('rhd,khd->hrk', g_heads, split_heads(value_rows), preferred_el...]
    all_to_all x9 -> x0, local copies, waits for them, and re-layouts: 11.5 us -> none  [the longest x2 2.43 us: body(): lax.all_to_all(g_audio, 'aud', split_axis=1, concat_axis=0, tiled=True)]
    convert_element_type x6 -> x0, other arithmetic: 8.12 us -> none  [the longest x1 1.97 us: body(): dk_aud.astype(jnp.bfloat16)]
    concatenate x13 -> x0, local copies, waits for them, and re-layouts: 8.03 us -> none  [nearby_row_span(): jnp.concatenate([pieces[window_shift] for window_shift in range(-reach_de...]
  transfers between devices with their start and end apart: 56 -> 0, of which waited for: 6 -> 0; matrix products, arithmetic and copies ran while one was open for 36% -> 0% of each run, Pallas kernels for 0% -> 0%
where the time goes in v1:
time: 70.5 us; the launch traced here: 70.1 us
  Pallas kernels  55.5 us (79%)
  local copies, waits for them, and re-layouts  13.9 us (20%)
    pallas_call x1, Pallas kernels, body(): pl.pallas_call(functools.partial(kernel, n), out_shape=(video, audio, vid...  55.5 us
    unnamed x27, local copies, waits for them, and re-layouts  13.9 us

profile of v1, /device:TPU:12, one launch (start us, length us, event | category | flops | bytes accessed | tf_op | source)
XLA Modules:
  0.0 70.1 jit_solution(6399477479878831256)
XLA Ops:
  0.6 0.0 copy-start.8
  0.6 0.8 %copy.18.win = s32[64,2]{1,0:T(8,128)S(1)} copy(s32[64,2]{0,1:T(2,128)} %param.18) | data formatting | bytes 1024 | tf_op args[8]
  1.4 0.0 copy-done.8
  1.4 0.0 copy-start
  1.4 1.0 %copy-done = bf16[256,768]{1,0:T(8,128)(2,1)S(1)} copy-done((bf16[256,768]{1,0:T(8,128)(2,1)S(1)}, bf16[256,768]{1,0:T(8,128)(2,1)}, u32[]{:S(2)}) %copy-start) | copy-done | bytes 393240
  2.4 0.0 copy-start.1
  2.4 1.0 %copy-done.1 = bf16[256,768]{1,0:T(8,128)(2,1)S(1)} copy-done((bf16[256,768]{1,0:T(8,128)(2,1)S(1)}, bf16[256,768]{1,0:T(8,128)(2,1)}, u32[]{:S(2)}) %copy-start.1) | copy-done | bytes 393240
  3.4 0.0 copy-start.2
  3.4 1.0 %copy-done.2 = bf16[256,768]{1,0:T(8,128)(2,1)S(1)} copy-done((bf16[256,768]{1,0:T(8,128)(2,1)S(1)}, bf16[256,768]{1,0:T(8,128)(2,1)}, u32[]{:S(2)}) %copy-start.2) | copy-done | bytes 393240
  4.4 0.0 copy-start.3
  4.4 1.0 %copy-done.3 = bf16[256,768]{1,0:T(8,128)(2,1)S(1)} copy-done((bf16[256,768]{1,0:T(8,128)(2,1)S(1)}, bf16[256,768]{1,0:T(8,128)(2,1)}, u32[]{:S(2)}) %copy-start.3) | copy-done | bytes 393240
  5.4 0.0 copy-start.4
  5.4 0.9 %copy-done.4 = bf16[32,1536]{1,0:T(8,128)(2,1)S(1)} copy-done((bf16[32,1536]{1,0:T(8,128)(2,1)S(1)}, bf16[32,1536]{1,0:T(8,128)(2,1)}, u32[]{:S(2)}) %copy-start.4) | copy-done | bytes 98328
  6.3 0.0 copy-start.5
  6.3 0.9 %copy-done.5 = bf16[32,1536]{1,0:T(8,128)(2,1)S(1)} copy-done((bf16[32,1536]{1,0:T(8,128)(2,1)S(1)}, bf16[32,1536]{1,0:T(8,128)(2,1)}, u32[]{:S(2)}) %copy-start.5) | copy-done | bytes 98328
  7.2 0.0 copy-start.6
  7.2 0.9 %copy-done.6 = bf16[32,1536]{1,0:T(8,128)(2,1)S(1)} copy-done((bf16[32,1536]{1,0:T(8,128)(2,1)S(1)}, bf16[32,1536]{1,0:T(8,128)(2,1)}, u32[]{:S(2)}) %copy-start.6) | copy-done | bytes 98328
  8.1 0.0 copy-start.7
  8.1 0.9 %copy-done.7 = bf16[32,1536]{1,0:T(8,128)(2,1)S(1)} copy-done((bf16[32,1536]{1,0:T(8,128)(2,1)S(1)}, bf16[32,1536]{1,0:T(8,128)(2,1)}, u32[]{:S(2)}) %copy-start.7) | copy-done | bytes 98328
  9.0 55.5 %shard_map.161 = (bf16[256,768]{1,0:T(8,128)(2,1)S(1)}, bf16[32,1536]{1,0:T(8,128)(2,1)S(1)}, bf16[256,768]{1,0:T(8,128)(2,1)S(1)}, bf16[256,768]{1,0:T(8,128)(2...) custom-call(s32[64,2]{1,0:T(8,128)S(1)} %copy.18.win, ...), custom_call_target="tpu_custom_call" | custom-call | tf_op jit(solution)/shard_map/pallas_call | solution.py:611
  64.5 0.7 %copy.27 = bf16[256,768]{1,0:T(8,128)(2,1)} copy(bf16[256,768]{1,0:T(8,128)(2,1)S(1)} %get-tuple-element.16) | data formatting | bytes 786432
  65.3 0.6 copy.28
  65.9 0.7 %copy.29 = bf16[256,768]{1,0:T(8,128)(2,1)} copy(bf16[256,768]{1,0:T(8,128)(2,1)S(1)} %get-tuple-element.18) | data formatting | bytes 786432
  66.7 0.7 %copy.30 = bf16[256,768]{1,0:T(8,128)(2,1)} copy(bf16[256,768]{1,0:T(8,128)(2,1)S(1)} %get-tuple-element.19) | data formatting | bytes 786432
  67.4 0.7 %copy.31 = bf16[256,768]{1,0:T(8,128)(2,1)} copy(bf16[256,768]{1,0:T(8,128)(2,1)S(1)} %get-tuple-element.20) | data formatting | bytes 786432
  68.2 0.6 copy.32
  68.8 0.6 copy.33
  69.4 0.6 copy.34
Async XLA Ops:
  0.6 0.8 %copy-start.8 = (s32[16]{0:T(128)S(1)}, s32[16]{0:T(128)}, u32[]{:S(2)}) copy-start(s32[16]{0:T(128)} %alen.1) | copy-start | bytes 196
  1.4 1.0 %copy-start = (bf16[256,768]{1,0:T(8,128)(2,1)S(1)}, bf16[256,768]{1,0:T(8,128)(2,1)}, u32[]{:S(2)}) copy-start(bf16[256,768]{1,0:T(8,128)(2,1)} %qv.1) | copy-start | bytes 1179652
  2.4 1.0 %copy-start.1 = (bf16[256,768]{1,0:T(8,128)(2,1)S(1)}, bf16[256,768]{1,0:T(8,128)(2,1)}, u32[]{:S(2)}) copy-start(bf16[256,768]{1,0:T(8,128)(2,1)} %kv.1) | copy-start | bytes 1179652
  3.4 1.0 %copy-start.2 = (bf16[256,768]{1,0:T(8,128)(2,1)S(1)}, bf16[256,768]{1,0:T(8,128)(2,1)}, u32[]{:S(2)}) copy-start(bf16[256,768]{1,0:T(8,128)(2,1)} %vv.1) | copy-start | bytes 1179652
  4.4 1.0 %copy-start.3 = (bf16[256,768]{1,0:T(8,128)(2,1)S(1)}, bf16[256,768]{1,0:T(8,128)(2,1)}, u32[]{:S(2)}) copy-start(bf16[256,768]{1,0:T(8,128)(2,1)} %gv.1) | copy-start | bytes 1179652
  5.4 0.9 %copy-start.4 = (bf16[32,1536]{1,0:T(8,128)(2,1)S(1)}, bf16[32,1536]{1,0:T(8,128)(2,1)}, u32[]{:S(2)}) copy-start(bf16[32,1536]{1,0:T(8,128)(2,1)} %qa.1) | copy-start | bytes 294916
  6.3 0.9 %copy-start.5 = (bf16[32,1536]{1,0:T(8,128)(2,1)S(1)}, bf16[32,1536]{1,0:T(8,128)(2,1)}, u32[]{:S(2)}) copy-start(bf16[32,1536]{1,0:T(8,128)(2,1)} %ka.1) | copy-start | bytes 294916
  7.2 0.9 %copy-start.6 = (bf16[32,1536]{1,0:T(8,128)(2,1)S(1)}, bf16[32,1536]{1,0:T(8,128)(2,1)}, u32[]{:S(2)}) copy-start(bf16[32,1536]{1,0:T(8,128)(2,1)} %va.1) | copy-start | bytes 294916
  8.1 0.9 %copy-start.7 = (bf16[32,1536]{1,0:T(8,128)(2,1)S(1)}, bf16[32,1536]{1,0:T(8,128)(2,1)}, u32[]{:S(2)}) copy-start(bf16[32,1536]{1,0:T(8,128)(2,1)} %ga.1) | copy-start | bytes 294916

commit v2 on v1

--- a/solution.py
+++ b/solution.py
@@ -16,6 +16,7 @@
 SLOTS = 2 * REACH + 1
 OWN = REACH
 PAIR = 2 * HD
+VMEM = 62 * 1024 * 1024
 
 F32 = jnp.float32
 BF16 = jnp.bfloat16
@@ -37,19 +38,19 @@
     n,
     win,
     alen,
-    qv,
-    kv,
-    vv,
-    gv,
+    qv_in,
+    kv_in,
+    vv_in,
+    gv_in,
     qa,
     ka,
     va,
     ga,
-    out_v,
+    out_v_hbm,
     out_a,
-    dq_v,
-    dk_v,
-    dv_v,
+    dq_v_hbm,
+    dk_v_hbm,
+    dv_v_hbm,
     dq_a,
     dk_a,
     dv_a,
@@ -67,6 +68,18 @@
     mate_in,
     far_in,
     fin,
+    qv,
+    kv,
+    vv,
+    gv,
+    out_v,
+    dq_v,
+    dk_v,
+    dv_v,
+    own_sem,
+    video_sem,
+    write_sem,
+    fin_sem,
     x_send,
     x_recv,
     far_send,
@@ -94,6 +107,7 @@
     half = qa.shape[0]
     width = qv.shape[1]
     vrows = qv.shape[0]
+    wide = width // 2
     arows = 2 * half
     vblocks = vrows // BLK
     heads = width // HD
@@ -129,10 +143,28 @@
             )
 
     ins = (qa, ga, ka, va)
-    own_cols = pl.ds(pl.multiple_of(a * width, width), width)
-    peer_cols = pl.ds(pl.multiple_of(peer * width, width), width)
-    for t in range(4):
-        near[t, rows(OWN, a, half), :] = ins[t][:, own_cols]
+    own_cols = pl.ds(pl.multiple_of(a * width, PAIR), width)
+    peer_cols = pl.ds(pl.multiple_of(peer * width, PAIR), width)
+    own_in = [
+        pltpu.make_async_copy(
+            ins[t].at[:, own_cols], near.at[t, rows(OWN, a, half)], own_sem.at[t]
+        )
+        for t in range(4)
+    ]
+    video_in = [
+        pltpu.make_async_copy(src, dst, video_sem.at[t])
+        for t, (src, dst) in enumerate(
+            ((kv_in, kv), (vv_in, vv), (qv_in, qv), (gv_in, gv))
+        )
+    ]
+    video_out = [
+        pltpu.make_async_copy(src, dst, write_sem.at[t])
+        for t, (src, dst) in enumerate(
+            ((out_v, out_v_hbm), (dq_v, dq_v_hbm), (dk_v, dk_v_hbm), (dv_v, dv_v_hbm))
+        )
+    ]
+    for copy in own_in + video_in:
+        copy.start()
 
     pl.semaphore_wait(barrier, 1 + sum(jnp.where(has[o], 1, 0) for o in has))
 
@@ -233,6 +265,8 @@
 
     x_copy[0].start()
     x_copy[1].start()
+    for copy in own_in:
+        copy.wait()
     send_own(0, 0)
     x_copy[2].start()
     x_copy[3].start()
@@ -323,6 +357,8 @@
             stats[...] = jnp.where(lane_s == head + 2 * heads, mixed, old)
         return carry
 
+    video_in[0].wait()
+    video_in[1].wait()
     lax.fori_loop(0, pairs, av_scores, 0)
 
     def stats_copy(o):
@@ -370,6 +406,8 @@
     take_and_relay(1, 0)
     take_and_relay(1, 1)
     finish_group(1)
+    video_in[2].wait()
+    video_in[3].wait()
 
     def store_part(kind, member, c, value):
         part[kind, member, :, c] = value
@@ -418,110 +456,117 @@
     )
     each(res_copy, lambda c: c.start())
 
-    lax.fori_loop(pairs // 2, pairs, va_all, 0)
-
-    def rm_copy(kind, to_owner, src_slot):
+
+    def part_of(hf):
+        return pl.ds(hf * wide, wide)
+
+    def rm_copy(kind, hf, to_owner, src_slot):
         span = pl.ds(pl.multiple_of(src_slot * arows, arows), arows)
         return remote(
-            sendb.at[kind, :, span],
-            mate_in.at[kind, to_owner],
-            rm_send.at[kind, to_owner],
-            rm_recv.at[kind, to_owner],
+            sendb.at[kind, :, span, part_of(hf)],
+            mate_in.at[kind, to_owner, :, :, part_of(hf)],
+            rm_send.at[kind, hf, to_owner],
+            rm_recv.at[kind, hf, to_owner],
             at(mate),
         )
 
-    def rf_copy(kind, side):
+    def rf_copy(kind, hf, side):
         slot = (0, 4)[side]
         return remote(
-            sendb.at[kind, :, pl.ds(slot * arows, arows)],
-            far_in.at[kind, 1 - side],
-            rf_send.at[kind, side],
-            rf_recv.at[kind, 1 - side],
+            sendb.at[kind, :, pl.ds(slot * arows, arows), part_of(hf)],
+            far_in.at[kind, 1 - side, :, :, part_of(hf)],
+            rf_send.at[kind, hf, side],
+            rf_recv.at[kind, hf, 1 - side],
             at(d + (-2, 2)[side]),
         )
 
-    def rf_arrived(kind, side):
-        return remote(
-            sendb.at[kind, :, pl.ds(0, arows)],
-            far_in.at[kind, side],
-            rf_send.at[kind, side],
-            rf_recv.at[kind, side],
+    def rf_arrived(kind, hf, side):
+        return remote(
+            sendb.at[kind, :, pl.ds(0, arows), part_of(hf)],
+            far_in.at[kind, side, :, :, part_of(hf)],
+            rf_send.at[kind, hf, side],
+            rf_recv.at[kind, hf, side],
             at(d + (-2, 2)[side]),
         )
 
-    def return_first(kind):
+    def return_first(kind, hf):
         @pl.when(relays_in)
         def _():
-            rm_copy(kind, 0, low_slot).start()
+            rm_copy(kind, hf, 0, low_slot).start()
 
         @pl.when((odd == 0) & has[-2])
         def _():
-            rf_copy(kind, 0).start()
+            rf_copy(kind, hf, 0).start()
 
         @pl.when((odd == 1) & has[2])
         def _():
-            rf_copy(kind, 1).start()
-
-        rm_copy(kind, 1, high_slot).start()
-
-    def return_second(kind):
+            rf_copy(kind, hf, 1).start()
+
+        rm_copy(kind, hf, 1, high_slot).start()
+
+    def return_second(kind, hf):
         for side, parity in ((1, 0), (0, 1)):
 
             @pl.when((odd == parity) & has[(-2, 2)[side]])
             def _(side=side):
-                rm_copy(kind, 0, low_slot).wait_recv()
+                rm_copy(kind, hf, 0, low_slot).wait_recv()
                 span = pl.ds((0, 4)[side] * arows, arows)
                 for member in range(2):
-                    sendb[kind, member, span, :] = (
-                        part[kind, member, span, :] + mate_in[kind, 0, member].astype(F32)
+                    sendb[kind, member, span, part_of(hf)] = (
+                        part[kind, member, span, part_of(hf)]
+                        + mate_in[kind, 0, member, :, part_of(hf)].astype(F32)
                     ).astype(BF16)
-                rf_copy(kind, side).start()
+                rf_copy(kind, hf, side).start()
 
     finals = ((dk_a, dv_a), (out_a, dq_a))
 
-    def xo_copy(kind, member):
-        return remote(
-            fin.at[kind, member, pl.ds(pl.multiple_of(peer * half, half), half)],
-            finals[kind][member].at[:, own_cols],
-            xo_send.at[kind, member],
-            xo_recv.at[kind, member],
+    def span_of(index, hf):
+        return pl.ds(pl.multiple_of(index * width + hf * wide, PAIR), wide)
+
+    def xo_copy(kind, hf, member, landing):
+        return remote(
+            fin.at[kind, member, pl.ds(pl.multiple_of(peer * half, half), half), part_of(hf)],
+            finals[kind][member].at[:, span_of(landing, hf)],
+            xo_send.at[kind, hf, member],
+            xo_recv.at[kind, hf, member],
             {"vid": d, "aud": peer},
         )
 
-    def xo_arrived(kind, member):
-        return remote(
-            fin.at[kind, member, pl.ds(pl.multiple_of(peer * half, half), half)],
-            finals[kind][member].at[:, peer_cols],
-            xo_send.at[kind, member],
-            xo_recv.at[kind, member],
-            {"vid": d, "aud": peer},
-        )
-
-    def return_last(kind):
-        rm_copy(kind, 1, high_slot).wait_recv()
+    def fin_copy(kind, hf, member):
+        return pltpu.make_async_copy(
+            fin.at[kind, member, pl.ds(pl.multiple_of(a * half, half), half), part_of(hf)],
+            finals[kind][member].at[:, span_of(a, hf)],
+            fin_sem.at[kind, hf, member],
+        )
+
+    def return_last(kind, hf):
+        rm_copy(kind, hf, 1, high_slot).wait_recv()
         for side in range(2):
 
             @pl.when(has[(-2, 2)[side]])
             def _(side=side):
-                rf_arrived(kind, side).wait_recv()
+                rf_arrived(kind, hf, side).wait_recv()
 
         for member in range(2):
             value = (
-                part[kind, member, own_span, :]
-                + mate_in[kind, 1, member].astype(F32)
-                + far_in[kind, 0, member].astype(F32)
-                + far_in[kind, 1, member].astype(F32)
+                part[kind, member, own_span, part_of(hf)]
+                + mate_in[kind, 1, member, :, part_of(hf)].astype(F32)
+                + far_in[kind, 0, member, :, part_of(hf)].astype(F32)
+                + far_in[kind, 1, member, :, part_of(hf)].astype(F32)
             )
             if kind == 1 and member == 0:
                 token = lax.broadcasted_iota(jnp.int32, value.shape, 0)
                 value = jnp.where(token < lens[OWN], value, 0.0)
-            fin[kind, member] = value.astype(BF16)
-            xo_copy(kind, member).start()
-            finals[kind][member][:, own_cols] = fin[
-                kind, member, pl.ds(pl.multiple_of(a * half, half), half), :
-            ]
-
-    return_first(0)
+            fin[kind, member, :, part_of(hf)] = value.astype(BF16)
+            xo_copy(kind, hf, member, a).start()
+            fin_copy(kind, hf, member).start()
+
+    return_first(0, 0)
+    lax.fori_loop(pairs // 2, pairs, va_all, 0)
+    video_out[0].start()
+    video_out[1].start()
+    return_first(0, 1)
+    return_second(0, 0)
     each(res_arrived, lambda c: c.wait_recv())
 
     def av_all(i, carry):
@@ -550,15 +595,23 @@
         return carry
 
     lax.fori_loop(0, pairs // 2, av_all, 0)
-    return_second(0)
+    return_first(1, 0)
+    return_second(0, 1)
     lax.fori_loop(pairs // 2, pairs, av_all, 0)
-    return_first(1)
-    return_second(1)
-    return_last(0)
-    return_last(1)
-    for kind in range(2):
+    return_first(1, 1)
+    video_out[2].start()
+    video_out[3].start()
+    return_second(1, 0)
+    return_second(1, 1)
+    order = ((0, 0), (0, 1), (1, 0), (1, 1))
+    for kind, hf in order:
+        return_last(kind, hf)
+    for kind, hf in order:
         for member in range(2):
-            xo_arrived(kind, member).wait_recv()
+            xo_copy(kind, hf, member, peer).wait_recv()
+            fin_copy(kind, hf, member).wait()
+    for copy in video_out:
+        copy.wait()
 
     for t in range(4):
         x_copy[t].wait_send()
@@ -578,21 +631,36 @@
 
     each(stats_copy, lambda c: c.wait_send())
     each(res_copy, lambda c: c.wait_send())
-    for kind in range(2):
+    for kind, hf in order:
 
         @pl.when(relays_in)
-        def _(kind=kind):
-            rm_copy(kind, 0, low_slot).wait_send()
-
-        rm_copy(kind, 1, high_slot).wait_send()
+        def _(kind=kind, hf=hf):
+            rm_copy(kind, hf, 0, low_slot).wait_send()
+
+        rm_copy(kind, hf, 1, high_slot).wait_send()
         for side in range(2):
 
             @pl.when(has[(-2, 2)[side]])
-            def _(kind=kind, side=side):
-                rf_copy(kind, side).wait_send()
+            def _(kind=kind, hf=hf, side=side):
+                rf_copy(kind, hf, side).wait_send()
 
         for member in range(2):
-            xo_copy(kind, member).wait_send()
+            xo_copy(kind, hf, member, a).wait_send()
+
+
+def write_out(*refs):
+    count = (len(refs) - 2) // 3
+    sources, results, held = (refs[k * count : (k + 1) * count] for k in range(3))
+    into, out = refs[-2:]
+    reads = [pltpu.make_async_copy(sources[t], held[t], into.at[t]) for t in range(count)]
+    writes = [pltpu.make_async_copy(held[t], results[t], out.at[t]) for t in range(count)]
+    for copy in reads:
+        copy.start()
+    for read, write in zip(reads, writes):
+        read.wait()
+        write.start()
+    for copy in writes:
+        copy.wait()
 
 
 def body(n, q_video, k_video, v_video, g_video, q_audio, k_audio, v_audio, g_audio, window, alen):
@@ -605,14 +673,15 @@
     video = jax.ShapeDtypeStruct((vrows, width), BF16)
     audio = jax.ShapeDtypeStruct((half, full), BF16)
     dma = pltpu.SemaphoreType.DMA
-    vmem = pl.BlockSpec(memory_space=pltpu.VMEM)
+    hbm = pl.BlockSpec(memory_space=pltpu.HBM)
     smem = pl.BlockSpec(memory_space=pltpu.SMEM)
-    sems = [(4,), (2, 2, 2), (2, 2), (2, 2), (SLOTS,), (SLOTS,), (2, 2), (2, 2), (2, 2)]
-    return pl.pallas_call(
+    sems = [(4,), (2, 2, 2), (2, 2), (2, 2), (SLOTS,), (SLOTS,)] + [(2, 2, 2)] * 3
+    outs = (video, audio, video, video, video, audio, audio, audio)
+    found = pl.pallas_call(
         functools.partial(kernel, n),
-        out_shape=(video, audio, video, video, video, audio, audio, audio),
-        in_specs=[smem] * 2 + [vmem] * 8,
-        out_specs=(vmem,) * 8,
+        out_shape=outs,
+        in_specs=[smem] * 2 + [hbm] * 8,
+        out_specs=(hbm,) * 8,
         scratch_shapes=[
             pltpu.VMEM((4, near_rows, width), BF16),
             pltpu.VMEM((heads, near_rows, vrows), F32),
@@ -629,11 +698,21 @@
             pltpu.VMEM((2, 2, 2, arows, width), BF16),
             pltpu.VMEM((2, 2, arows, width), BF16),
         ]
+        + [pltpu.VMEM((vrows, width), BF16)] * 8
+        + [dma((4,)), dma((4,)), dma((4,)), dma((2, 2, 2))]
         + [dma(shape) for shape in sems for _ in range(2)],
         compiler_params=pltpu.CompilerParams(
-            collective_id=0, has_side_effects=True, vmem_limit_bytes=48 * 1024 * 1024
+            collective_id=0, has_side_effects=True, vmem_limit_bytes=VMEM
         ),
     )(window, alen, q_video, k_video, v_video, g_video, q_audio, k_audio, v_audio, g_audio)
+    return pl.pallas_call(
+        write_out,
+        out_shape=outs,
+        in_specs=[hbm] * 8,
+        out_specs=(hbm,) * 8,
+        scratch_shapes=[pltpu.VMEM(x.shape, BF16) for x in outs] + [dma((8,)), dma((8,))],
+        compiler_params=pltpu.CompilerParams(vmem_limit_bytes=VMEM),
+    )(*found)
 
 
 def solution(mesh):

time: 70.5 us -> 58.5 us (0.83)
  local copies, waits for them, and re-layouts: 13.9 us -> 1.38 us
    unnamed x27 -> x1, local copies, waits for them, and re-layouts: 13.9 us -> 1.38 us
    pallas_call x1 -> x2, Pallas kernels: 55.5 us -> 56.2 us  [the longest x1 53.8 us: body(): pl.pallas_call(functools.partial(kernel, n), out_shape=outs, in_specs=[sm...]
where the time goes in v2:
time: 58.5 us; the launch traced here: 58.2 us
  Pallas kernels  56.2 us (96%)
  local copies, waits for them, and re-layouts  1.38 us (2%)
  between operations  0.64 us (1%)
    pallas_call x1, Pallas kernels, body(): pl.pallas_call(functools.partial(kernel, n), out_shape=outs, in_specs=[sm...  53.8 us
    pallas_call x1, Pallas kernels, body(): pl.pallas_call(write_out, out_shape=outs, in_specs=[hbm] * 8, out_specs=(...  2.4 us
    unnamed x1, local copies, waits for them, and re-layouts  1.38 us

profile of v2, /device:TPU:12, one launch (start us, length us, event | category | flops | bytes accessed | tf_op | source)
XLA Modules:
  0.0 58.2 jit_solution(8026561268270140311)
XLA Ops:
  0.6 1.4 %copy.18.win = s32[64,2]{1,0:T(8,128)} copy(s32[64,2]{0,1:T(2,128)} %param.18) | data formatting | bytes 1024 | tf_op args[8]
  2.0 53.8 %shard_map.161 = (bf16[256,768]{1,0:T(8,128)(2,1)}, bf16[32,1536]{1,0:T(8,128)(2,1)}, bf16[256,768]{1,0:T(8,128)(2,1)}, bf16[256,768]{1,0:T(8,128)(2,1)}, bf16[2...) custom-call(s32[64,2]{1,0:T(8,128)} %copy.18.win, ...), custom_call_target="tpu_custom_call" | custom-call | tf_op jit(solution)/shard_map/pallas_call | solution.py:680
  55.8 2.4 %shard_map.162 = (bf16[256,768]{1,0:T(8,128)(2,1)}, bf16[32,1536]{1,0:T(8,128)(2,1)}, bf16[256,768]{1,0:T(8,128)(2,1)}, bf16[256,768]{1,0:T(8,128)(2,1)}, bf16[2...) custom-call(bf16[256,768]{1,0:T(8,128)(2,1)} %get-tuple-element.16.refs_0_, ...), custom_call_target="tpu_custom_call" | custom-call | tf_op jit(solution)/shard_map/pallas_call | solution.py:708

commit v3 on v2

--- a/solution.py
+++ b/solution.py
@@ -163,7 +163,7 @@
             ((out_v, out_v_hbm), (dq_v, dq_v_hbm), (dk_v, dk_v_hbm), (dv_v, dv_v_hbm))
         )
     ]
-    for copy in own_in + video_in:
+    for copy in own_in:
         copy.start()
 
     pl.semaphore_wait(barrier, 1 + sum(jnp.where(has[o], 1, 0) for o in has))
@@ -265,11 +265,16 @@
 
     x_copy[0].start()
     x_copy[1].start()
-    for copy in own_in:
-        copy.wait()
+    own_in[0].wait()
+    own_in[1].wait()
     send_own(0, 0)
     x_copy[2].start()
     x_copy[3].start()
+    own_in[2].wait()
+    own_in[3].wait()
+    send_own(1, 0)
+    for copy in video_in:
+        copy.start()
 
     for slot in range(SLOTS):
         o = slot - OWN
@@ -322,7 +327,6 @@
     x_arrived(0).wait_recv()
     x_arrived(1).wait_recv()
     send_own(0, 1)
-    send_own(1, 0)
     take_and_relay(0, 0)
     x_arrived(2).wait_recv()
     x_arrived(3).wait_recv()

time: 58.5 us -> 59.6 us (1.019)
  Pallas kernels: 56.2 us -> 57.3 us
    pallas_call x1, Pallas kernels: 53.8 us -> 54.9 us  [body(): pl.pallas_call(functools.partial(kernel, n), out_shape=outs, in_specs=[sm...]
where the time goes in v3:
time: 59.6 us; the launch traced here: 59.3 us
  Pallas kernels  57.3 us (96%)
  local copies, waits for them, and re-layouts  1.38 us (2%)
  between operations  0.64 us (1%)
    pallas_call x1, Pallas kernels, body(): pl.pallas_call(functools.partial(kernel, n), out_shape=outs, in_specs=[sm...  54.9 us
    pallas_call x1, Pallas kernels, body(): pl.pallas_call(write_out, out_shape=outs, in_specs=[hbm] * 8, out_specs=(...  2.4 us
    unnamed x1, local copies, waits for them, and re-layouts  1.38 us

profile of v3, /device:TPU:12, one launch (start us, length us, event | category | flops | bytes accessed | tf_op | source)
XLA Modules:
  0.0 59.3 jit_solution(868265378817453239)
XLA Ops:
  0.6 1.4 %copy.18.win = s32[64,2]{1,0:T(8,128)} copy(s32[64,2]{0,1:T(2,128)} %param.18) | data formatting | bytes 1024 | tf_op args[8]
  2.0 54.9 %shard_map.161 = (bf16[256,768]{1,0:T(8,128)(2,1)}, bf16[32,1536]{1,0:T(8,128)(2,1)}, bf16[256,768]{1,0:T(8,128)(2,1)}, bf16[256,768]{1,0:T(8,128)(2,1)}, bf16[2...) custom-call(s32[64,2]{1,0:T(8,128)} %copy.18.win, ...), custom_call_target="tpu_custom_call" | custom-call | tf_op jit(solution)/shard_map/pallas_call | solution.py:684
  56.9 2.4 %shard_map.162 = (bf16[256,768]{1,0:T(8,128)(2,1)}, bf16[32,1536]{1,0:T(8,128)(2,1)}, bf16[256,768]{1,0:T(8,128)(2,1)}, bf16[256,768]{1,0:T(8,128)(2,1)}, bf16[2...) custom-call(bf16[256,768]{1,0:T(8,128)(2,1)} %get-tuple-element.16.refs_0_, ...), custom_call_target="tpu_custom_call" | custom-call | tf_op jit(solution)/shard_map/pallas_call | solution.py:712
